TPU v7x, 32 devices: a whole 2x2x4 slice. The times are simulated.
32 devices in a mesh: member: 2 (over x), lon: 16 (over z, y, core).
Axes of the slice: x: 2, y: 2, z: 4, core: 2. Of those that a mesh axis runs over, the one named last changes fastest.
Arguments:
- obs_departure: bfloat16 [8192], P(('member', 'lon')), parts along dimension 0, may hold values from -6 to 6
- obs_precision: bfloat16 [4096], P('lon'), may hold values from 0.25 to 4
- obs_columns: int32 [4096], P('lon'), may hold values from 0 to 8191, as said below
- obs_counts: int32 [16], P('lon'), may hold values from 128 to 256, as said below
- obs_blocks: int32 [4096], P('lon'), may hold values from 0 to 63
- weight_table: bfloat16 [1024, 192], P('lon'), may hold values from -0.4375 to 0.4375
- lon_coeff: float32 [32, 64, 128], P(None, 'lon'), may hold values from 0.02 to 0.12
- lat_coeff: float32 [32, 64, 128], P(None, 'lon'), may hold values from 0.02 to 0.12
- vert_coeff: float32 [32, 64, 128], P(None, 'lon'), may hold values from 0.5 to 20
Outputs:
- control: float32 [12, 32, 64, 128], P('member', None, 'lon'), parts along dimension 0
- increment: float32 [12, 32, 64, 128], P('member', None, 'lon'), parts along dimension 0
- obs_fit: float32 [8192], P(('member', 'lon')), parts along dimension 0
There are 2 independent parts, one for each index of `member`. A program takes and returns all parts, laid end to end along the dimension named above; an argument that names none is the same for every part. Nothing has to cross between parts.
Inputs may be any that keep to these rules, and one draw needn't show every extreme that they name: `obs_columns`: only live slots are read; dead slots hold valid column numbers. The live observations of one device put at most 32 into the columns of any one device (a block of 4 longitudes), and in every draw one device takes exactly 32 from every device. The live slots of a device are its first obs_counts ones; some device is full. `obs_blocks`: A row of the device's own part of weight_table.
All inputs are finite; a program needn't handle non-finite values.
Results may differ from a plain program's by a relative error of at most 0.0003.
Values may be sent and summed in bfloat16 or wider, within the bound.
A program may use at most 64 MiB of HBM per device.

v0:
```python
import jax
import jax.numpy as jnp
from jax import lax
from jax.sharding import PartitionSpec as P

VARS = 6
LEV = 32
STEPS = 2
EXACT = lax.Precision.HIGHEST


def neighbours(block, axis):
    count = lax.axis_size(axis)
    up = [(i, (i + 1) % count) for i in range(count)]
    down = [(target, source) for source, target in up]
    return lax.ppermute(block, axis, up), lax.ppermute(block, axis, down)


def shifted(field, stride, fill):
    widths = [(0, 0)] * field.ndim
    widths[-2] = (max(stride, 0), max(-stride, 0))
    padded = jnp.pad(field, widths, constant_values=fill)
    first = max(-stride, 0)
    return lax.slice_in_dim(padded, first, first + field.shape[-2], axis=field.ndim - 2)


def factor_vertical(vert):
    levels = vert.shape[-2]
    inner = (jnp.arange(levels) < levels - 1)[:, None]
    upward = jnp.where(inner, vert, 0.0)
    downward = shifted(upward, 1, 0.0)
    lower, upper = -downward, -upward
    diag = 1.0 + downward + upward
    factors = []
    stride = 1
    while stride < levels:
        alpha = -lower / shifted(diag, stride, 1.0)
        gamma = -upper / shifted(diag, -stride, 1.0)
        new_lower = alpha * shifted(lower, stride, 0.0)
        new_upper = gamma * shifted(upper, -stride, 0.0)
        diag = diag + alpha * shifted(upper, stride, 0.0) + gamma * shifted(lower, -stride, 0.0)
        factors.append((stride, alpha, gamma))
        lower, upper = new_lower, new_upper
        stride *= 2
    return factors, 1.0 / diag


def solve_vertical(factored, field, first, count):
    factors, scale = factored
    for stride, alpha, gamma in factors:
        alpha, gamma = alpha[first : first + count], gamma[first : first + count]
        field = field + alpha * shifted(field, stride, 0.0) + gamma * shifted(field, -stride, 0.0)
    return field * scale[first : first + count]


def smooth(field, along, across, first):
    for _ in range(STEPS):
        count = field.shape[1]
        flux_lon = along[first : first + count - 1] * (field[:, 1:] - field[:, :-1])
        middle = field[:, 1:-1]
        flux_lat = across[first + 1 : first + count - 1] * (jnp.roll(middle, -1, -1) - middle)
        field = middle + flux_lon[:, 1:] - flux_lon[:, :-1] + flux_lat - jnp.roll(flux_lat, 1, -1)
        first += 1
    return field


def on_device(
    obs_departure,
    obs_precision,
    obs_columns,
    obs_counts,
    obs_blocks,
    weight_table,
    lon_coeff,
    lat_coeff,
    vert_coeff,
):
    devices = lax.axis_size("lon")
    me = lax.axis_index("lon")
    levels, width, nlat = lon_coeff.shape
    percol = width * nlat
    depth = VARS * LEV
    per_dev = obs_columns.shape[0]
    capacity = max(per_dev // 64, 2 * ((per_dev + devices - 1) // devices))
    slots_all = devices * capacity
    bf16, f32 = jnp.bfloat16, jnp.float32

    open_face = jnp.arange(nlat) < nlat - 1
    coeffs = jnp.stack([lon_coeff, jnp.where(open_face, lat_coeff, 0.0), vert_coeff])
    coeffs = coeffs.transpose(0, 2, 1, 3)
    below, above = neighbours(coeffs, "lon")
    along, across, vert = jnp.concatenate([below, coeffs, above], axis=1)
    factored = factor_vertical(vert)

    slot = jnp.arange(per_dev, dtype=jnp.int32)
    live = slot < obs_counts[0]
    owner = obs_columns // percol
    local_col = obs_columns - owner * percol
    hits = (owner[:, None] == jnp.arange(devices, dtype=jnp.int32)) & live[:, None]
    before = jnp.dot(
        (slot[:, None] > slot).astype(bf16), hits.astype(bf16), preferred_element_type=f32
    )
    rank = jnp.sum(jnp.where(hits, before, 0.0), axis=1).astype(jnp.int32)
    target = jnp.where(live, owner * capacity + rank, slots_all)
    place = jnp.arange(slots_all, dtype=jnp.int32)[:, None] == target
    rows = weight_table.shape[0]
    pick = (obs_blocks[:, None] == jnp.arange(rows, dtype=jnp.int32)).astype(bf16)
    block_rows = jnp.dot(pick, weight_table, preferred_element_type=f32).astype(bf16)
    extra = jnp.stack(
        [
            obs_precision,
            obs_departure,
            (local_col // 16).astype(bf16),
            (local_col % 16).astype(bf16),
        ],
        axis=1,
    )
    payload = jnp.concatenate([block_rows, extra], axis=1)
    payload = jnp.dot(place.astype(bf16), payload, preferred_element_type=f32).astype(bf16)
    mine = lax.all_to_all(payload, "lon", split_axis=0, concat_axis=0, tiled=True)
    left, right = neighbours(mine, "lon")
    held = jnp.stack([left, mine, right])
    weights = held[..., :depth].astype(f32)
    precision = held[..., depth].astype(f32)
    departure = held[..., depth + 1].astype(f32)
    column = held[..., depth + 2].astype(jnp.int32) * 16 + held[..., depth + 3].astype(jnp.int32)
    at_column = column[..., None] == jnp.arange(percol, dtype=jnp.int32)
    own_precision = precision[1]

    def forward(field):
        flat = field.transpose(0, 2, 1, 3).reshape(depth, percol)
        dots = jnp.dot(weights[1], flat, precision=EXACT)
        return jnp.sum(jnp.where(at_column[1], dots, 0.0), axis=1)

    def adjoint(values):
        spread = jnp.where(at_column, values[..., None], 0.0)
        flat = jnp.einsum("bsc,bsn->cbn", weights, spread, precision=EXACT)
        return (
            flat.reshape(VARS, levels, 3 * width, nlat).transpose(0, 2, 1, 3)
        )

    def root(field):
        return solve_vertical(factored, smooth(field, along, across, STEPS), width, width)

    def root_adjoint(field):
        return smooth(solve_vertical(factored, field, 0, 3 * width), along, across, 0)

    def own(field):
        return field[:, STEPS : STEPS + width]

    rhs = root_adjoint(adjoint(precision * departure))
    rhs_own = own(rhs)
    rhs_root = root(rhs)
    rhs_obs = forward(rhs_root)
    weighted = own_precision * rhs_obs
    sums = jnp.stack([jnp.sum(rhs_own * rhs_own), jnp.sum(weighted * rhs_obs)])
    message = jnp.concatenate([weighted, sums])
    message = jnp.broadcast_to(message, (devices, slots_all + 2))
    message = lax.all_to_all(message, "lon", split_axis=0, concat_axis=0, tiled=True)
    norm, fit_norm = jnp.sum(message[:, slots_all:], axis=0)
    around = jnp.stack([(me + devices - 1) % devices, me, (me + 1) % devices])
    image = rhs + root_adjoint(adjoint(message[around, :slots_all]))
    alpha = norm / (norm + fit_norm)
    residual = rhs - alpha * image
    residual_own = own(residual)
    residual_root = root(residual)
    residual_obs = forward(residual_root)
    weighted = own_precision * residual_obs
    sums = jnp.stack(
        [
            jnp.sum(residual_own * residual_own),
            jnp.sum(residual_own * rhs_own),
            jnp.sum(weighted * residual_obs),
            jnp.sum(weighted * rhs_obs),
        ]
    )
    message = jnp.concatenate(
        [
            rhs_obs.reshape(devices, capacity),
            residual_obs.reshape(devices, capacity),
            jnp.broadcast_to(sums, (devices, 4)),
        ],
        axis=1,
    )
    message = lax.all_to_all(message, "lon", split_axis=0, concat_axis=0, tiled=True)
    fresh, cross, fit_fresh, fit_cross = jnp.sum(message[:, 2 * capacity :], axis=0)
    beta = fresh / norm
    curve = (
        fresh + fit_fresh + 2.0 * beta * (cross + fit_cross) + beta * beta * (norm + fit_norm)
    )
    second = fresh / curve
    first = alpha + second * beta
    control = first * rhs_own + second * residual_own
    increment = first * rhs_root + second * residual_root
    fit = first * message[:, :capacity] + second * message[:, capacity : 2 * capacity]
    fit = jnp.dot(fit.reshape(1, slots_all), place.astype(f32), precision=EXACT)[0]
    obs_fit = jnp.where(live, fit - obs_departure.astype(f32), 0.0)
    return control.transpose(0, 2, 1, 3), increment.transpose(0, 2, 1, 3), obs_fit


def solution(mesh):
    in_specs = (
        P(("member", "lon")),
        P("lon"),
        P("lon"),
        P("lon"),
        P("lon"),
        P("lon", None),
        P(None, "lon", None),
        P(None, "lon", None),
        P(None, "lon", None),
    )
    out_specs = (
        P("member", None, "lon", None),
        P("member", None, "lon", None),
        P(("member", "lon")),
    )
    return jax.shard_map(
        on_device, mesh=mesh, in_specs=in_specs, out_specs=out_specs, check_vma=False
    )
```

profile of v0, /device:TPU:0, one launch (start us, length us, event | category | flops | bytes accessed | tf_op | source)
XLA Modules:
  0.0 138.9 jit_solution(17466147372352237654)
XLA Ops:
  0.7 0.9 select_bitcast_fusion
  1.5 0.9 maximum_bitcast_fusion
  2.9 5.1 %collective-permute-start.3 = (f32[3,4,32,128]{3,1,2,0:T(4,128)S(1)}, f32[3,4,32,128]{3,1,2,0:T(4,128)S(1)}, u32[]{:S(2)}, u32[]{:S(2)}) collective-permute-start(f32[3,4,32,128]{3,1,2,0:T(4,128)S(1)} %maximum_bitcast_fusion), channel_id=1, source_target_pairs={{1,0},{2,1},{3,2},{4,3},{5,4},{6,5},{7,6},{8,7},{9,8},{10,9},{11,1... | collective-permute-start | bytes 589832 | tf_op jit(solution)/shard_map/ppermute | solution.py:16
  11.6 1.0 convolution_convert_fusion.1
  12.9 0.8 copy.34
  13.7 3.6 %all-to-all-start = ((bf16[16,32,196]{2,1,0:T(8,128)(2,1)}), bf16[16,32,196]{2,1,0:T(8,128)(2,1)S(1)}, u32[]{:S(2)}, u32[]{:S(2)}) async-start(bf16[16,32,196]{2,1,0:T(8,128)(2,1)} %bitcast.1), calls=%async_computation | async-start | bytes 524288 | tf_op jit(solution)/shard_map/all_to_all | solution.py:120
  31.0 4.0 %collective-permute-start.1 = (bf16[512,196]{0,1:T(8,128)(2,1)S(1)}, bf16[512,196]{0,1:T(8,128)(2,1)S(1)}, u32[]{:S(2)}, u32[]{:S(2)}) collective-permute-start(bf16[512,196]{0,1:T(8,128)(2,1)S(1)} %copy.35), channel_id=1, source_target_pairs={{1,0},{2,1},{3,2},{4,3},{5,4},{6,5},{7,6},{8,7},{9,8},{10,9},{11,1... | collective-permute-start | bytes 602120 | tf_op jit(solution)/shard_map/ppermute | solution.py:16
  36.0 2.5 %collective-permute-done = bf16[512,196]{0,1:T(8,128)(2,1)S(1)} collective-permute-done((bf16[512,196]{0,1:T(8,128)(2,1)S(1)}, bf16[512,196]{0,1:T(8,128)(2,1)S(1)}, u32[]{:S(2)}, u32[]{:S(2)}) %collective-permute-start) | collective-permute-done | bytes 200736 | tf_op jit(solution)/shard_map/ppermute | solution.py:16
  39.3 2.2 %fusion.62 = f32[192,3,512]{2,0,1:T(8,128)S(1)} fusion(f32[3,512]{1,0:T(4,128)S(1)} %bitcast.146, s32[3,512]{1,0:T(4,128)S(1)} %bitcast.142, bf16[1,512,196]{1,2,0:T(8,128)(2,1)S(1)} %bitcast.132, bf16[1,512,196]{1,2,0:T(8,128)(2,1)S(1)} %copy.37, bf16[1,512,196]{1,2,0:T(8,128)(2,1)S(1)} %bitcast.128), kind=kOutput, calls=%fused_computation.94 | convolution fusion | flops 1815281664 | bytes 1794048 | tf_op jit(solution)/shard_map/bsc,bsn->cbn/dot_general | solution.py:137
  42.3 0.9 reshape.213
  43.2 1.3 fusion.6
  58.5 0.9 multiply_reduce_fusion.2
  64.3 1.4 pad_maximum_fusion.6
  66.4 5.6 %all-to-all-start.1 = ((f32[16,1,514]{2,1,0:T(1,128)}), f32[16,1,514]{2,1,0:T(1,128)S(1)}, u32[]{:S(2)}, u32[]{:S(2)}) async-start(f32[16,1,514]{2,1,0:T(1,128)} %broadcast_in_dim.66), calls=%async_computation.1 | async-start | bytes 81920 | tf_op jit(solution)/shard_map/all_to_all | solution.py:159
  72.2 6.5 %all-to-all-done.1 = f32[16,1,514]{2,1,0:T(1,128)S(1)} async-done(((f32[16,1,514]{2,1,0:T(1,128)}), f32[16,1,514]{2,1,0:T(1,128)S(1)}, u32[]{:S(2)}, u32[]{:S(2)}) %all-to-all-start.1) | async-done | bytes 32928 | tf_op jit(solution)/shard_map/all_to_all | solution.py:159
  78.7 6.3 %while.1 = (s32[]{:T(128)}, f32[16,514]{1,0:T(8,128)S(1)}, s32[3,2]{0,1:T(2,128)S(1)}, f32[3,512]{1,0:T(4,128)S(1)}, s32[]{:T(128)}, /*index=5*/s32[]{:T(128)}) while((s32[]{:T(128)}, f32[16,514]{1,0:T(8,128)S(1)}, s32[3,2]{0,1:T(2,128)S(1)}, f32[3,512]{1,0:T(4,128)S(1)}, s32[]{:T(128)}, /*index=5*/s32[]{:T(128)}) %tuple.56), condition=%wide.while_cond, body=%wide.while_body.sunk | while | flops 2 | bytes 8305 | solution.py:162
  79.4 1.4 %dynamic-slice.7 = f32[1,512]{1,0:T(1,128)S(1)} dynamic-slice(f32[16,514]{1,0:T(8,128)S(1)} %get-tuple-element.112, s32[]{:T(128)} %bitcast.106, s32[]{:T(128)} %bitcast.107), dynamic_slice_sizes={1,512} | dynamic-slice | bytes 4100 | tf_op jit(solution)/shard_map/gather
  81.5 1.4 %dynamic-slice.7 = f32[1,512]{1,0:T(1,128)S(1)} dynamic-slice(f32[16,514]{1,0:T(8,128)S(1)} %get-tuple-element.112, s32[]{:T(128)} %bitcast.106, s32[]{:T(128)} %bitcast.107), dynamic_slice_sizes={1,512} | dynamic-slice | bytes 4100 | tf_op jit(solution)/shard_map/gather
  83.6 1.4 %dynamic-slice.7 = f32[1,512]{1,0:T(1,128)S(1)} dynamic-slice(f32[16,514]{1,0:T(8,128)S(1)} %get-tuple-element.112, s32[]{:T(128)} %bitcast.106, s32[]{:T(128)} %bitcast.107), dynamic_slice_sizes={1,512} | dynamic-slice | bytes 4100 | tf_op jit(solution)/shard_map/gather
  85.1 2.2 %fusion.65 = f32[192,3,512]{2,0,1:T(8,128)S(1)} fusion(f32[3,512]{1,0:T(4,128)S(1)} %get-tuple-element.10, s32[3,512]{1,0:T(4,128)S(1)} %bitcast.144, bf16[1,512,196]{1,2,0:T(8,128)(2,1)S(1)} %bitcast.133, bf16[1,512,196]{1,2,0:T(8,128)(2,1)S(1)} %copy-done.38, bf16[1,512,196]{1,2,0:T(8,128)(2,1)S(1)} %bitcast.129), kind=kOutput, calls=%fused_computation.95 | convolution fusion | flops 1815281664 | bytes 1794048 | tf_op jit(solution)/shard_map/bsc,bsn->cbn/dot_general | solution.py:137
  87.3 2.0 %copy.41 = f32[192,3,512]{2,1,0:T(4,128)} copy(f32[192,3,512]{2,0,1:T(8,128)S(1)} %fusion.65) | data formatting | bytes 2359296 | tf_op jit(solution)/shard_map/bsc,bsn->cbn/transpose | solution.py:137
  89.3 2.6 %reshape.216 = f32[6,32,12,128]{3,2,1,0:T(8,128)S(1)} reshape(f32[192,3,512]{2,1,0:T(4,128)} %copy.41) | data formatting | bytes 2359296 | tf_op jit(solution)/shard_map/reshape | solution.py:139
  91.9 1.3 fusion.10
  100.4 1.4 %fusion.46 = f32[6,9,32,128]{3,1,2,0:T(8,128)} fusion(f32[6,10,32,128]{3,1,2,0:T(8,128)S(1)} %fusion.48, f32[9,32,128]{2,0,1:T(8,128)S(1)} %copy-done.36), kind=kLoop, calls=%fused_computation.69 | loop fusion | flops 442368 | bytes 2801664 | tf_op jit(solution)/shard_map/mul | solution.py:59
  102.1 1.0 slice.857
  105.7 1.4 %fusion.88 = f32[6,8,32,128]{3,1,2,0:T(8,128)S(1)} fusion(f32[6,8,32,1]{3,1,2,0:T(8,128)} %slice.857, f32[6,8,32,127]{3,1,2,0:T(8,128)S(1)} %slice.856, f32[6,10,32,128]{3,1,2,0:T(8,128)S(1)} %fusion.48, f32[8,32,128]{2,0,1:T(8,128)S(1)} %copy-done.42), kind=kLoop, calls=%fused_computation.138 | loop fusion | flops 589824 | bytes 2490368 | tf_op jit(solution)/shard_map/mul | solution.py:61
  107.4 1.1 copy-done.2
  109.0 0.9 multiply_reduce_fusion.1
  117.4 1.7 %fusion.69 = f32[512]{0:T(512)S(1)} fusion(pred[3,512,512]{1,2,0:T(32,128)(4,1)} %copy-done.55, f32[24,8,4,128]{3,2,1,0:T(4,128)S(1)} %bitcast.134, bf16[1,512,196]{2,1,0:T(8,128)(2,1)S(1)} %bitcast.125), kind=kOutput, calls=%fused_computation.99 | convolution fusion | flops 604503552 | bytes 858112 | tf_op jit(solution)/shard_map/dot_general | solution.py:132
  119.8 2.6 %pad_maximum_fusion.7 = f32[68]{0:T(128)S(1)} fusion(f32[1]{0:T(128)} %bitcast.37, f32[1]{0:T(128)} %bitcast.36, f32[1]{0:T(128)} %bitcast.35, f32[1]{0:T(128)} %bitcast.34), kind=kLoop, calls=%fused_computation.358 | loop fusion | flops 204 | bytes 288 | tf_op jit(solution)/shard_map/stack | solution.py:169
  122.4 9.0 %all_to_all.33 = f32[16,1,68]{2,1,0:T(1,128)S(1)} all-to-all(f32[16,1,68]{2,1,0:T(1,128)S(1)} %bitcast.145), channel_id=1, replica_groups=mesh['member'=2,'lon'=16] {'lon'}, dimensions={0} | all-to-all | bytes 8704 | tf_op jit(solution)/shard_map/all_to_all | solution.py:185
  136.6 1.3 add_bitcast_fusion
  (298 shorter events, 59.8 us)
Async XLA Ops:
  0.6 11.0 %copy-start = (bf16[64,192]{1,0:T(8,128)(2,1)S(1)}, bf16[64,192]{1,0:T(8,128)(2,1)}, u32[]{:S(2)}) copy-start(bf16[64,192]{1,0:T(8,128)(2,1)} %param.14) | copy-start | bytes 73732
  2.4 15.6 %collective-permute-start.2 = (f32[3,4,32,128]{3,1,2,0:T(4,128)S(1)}, f32[3,4,32,128]{3,1,2,0:T(4,128)S(1)}, u32[]{:S(2)}, u32[]{:S(2)}) collective-permute-start(f32[3,4,32,128]{3,1,2,0:T(4,128)S(1)} %maximum_bitcast_fusion), channel_id=1, source_target_pairs={{0,1},{1,2},{2,3},{3,4},{4,5},{5,6},{6,7},{7,8},{8,9},{9,10},{10,1... | collective-permute-start | bytes 589832 | tf_op jit(solution)/shard_map/ppermute | solution.py:16
  2.9 15.1 %collective-permute-start.3 = (f32[3,4,32,128]{3,1,2,0:T(4,128)S(1)}, f32[3,4,32,128]{3,1,2,0:T(4,128)S(1)}, u32[]{:S(2)}, u32[]{:S(2)}) collective-permute-start(f32[3,4,32,128]{3,1,2,0:T(4,128)S(1)} %maximum_bitcast_fusion), channel_id=1, source_target_pairs={{1,0},{2,1},{3,2},{4,3},{5,4},{6,5},{7,6},{8,7},{9,8},{10,9},{11,1... | collective-permute-start | bytes 589832 | tf_op jit(solution)/shard_map/ppermute | solution.py:16
  13.7 16.6 %all-to-all-start = ((bf16[16,32,196]{2,1,0:T(8,128)(2,1)}), bf16[16,32,196]{2,1,0:T(8,128)(2,1)S(1)}, u32[]{:S(2)}, u32[]{:S(2)}) async-start(bf16[16,32,196]{2,1,0:T(8,128)(2,1)} %bitcast.1), calls=%async_computation | async-start | bytes 524288 | tf_op jit(solution)/shard_map/all_to_all | solution.py:120
  21.2 1.5 %copy-start.15 = (f32[12,32,128]{2,0,1:T(8,128)}, f32[12,32,128]{2,0,1:T(8,128)S(1)}, u32[]{:S(2)}) copy-start(f32[12,32,128]{2,0,1:T(8,128)S(1)} %get-tuple-element.41) | copy-start | bytes 589828
  21.2 3.0 %copy-start.16 = (f32[12,32,128]{2,0,1:T(8,128)}, f32[12,32,128]{2,0,1:T(8,128)S(1)}, u32[]{:S(2)}) copy-start(f32[12,32,128]{2,0,1:T(8,128)S(1)} %get-tuple-element.51) | copy-start | bytes 589828
  22.8 1.5 %copy-start.3 = (f32[12,32,128]{2,0,1:T(8,128)}, f32[12,32,128]{2,0,1:T(8,128)S(1)}, u32[]{:S(2)}) copy-start(f32[12,32,128]{2,0,1:T(8,128)S(1)} %get-tuple-element.57) | copy-start | bytes 589828
  24.3 1.6 %copy-start.5 = (f32[12,32,128]{2,0,1:T(8,128)}, f32[12,32,128]{2,0,1:T(8,128)S(1)}, u32[]{:S(2)}) copy-start(f32[12,32,128]{2,0,1:T(8,128)S(1)} %get-tuple-element.33) | copy-start | bytes 589828
  24.3 1.6 %copy-start.7 = (f32[12,32,128]{2,0,1:T(8,128)}, f32[12,32,128]{2,0,1:T(8,128)S(1)}, u32[]{:S(2)}) copy-start(f32[12,32,128]{2,0,1:T(8,128)S(1)} %get-tuple-element.55) | copy-start | bytes 589828
  25.9 1.6 %copy-start.9 = (f32[12,32,128]{2,0,1:T(8,128)}, f32[12,32,128]{2,0,1:T(8,128)S(1)}, u32[]{:S(2)}) copy-start(f32[12,32,128]{2,0,1:T(8,128)S(1)} %get-tuple-element.31) | copy-start | bytes 589828
  25.9 1.6 %copy-start.12 = (f32[12,32,128]{2,0,1:T(8,128)}, f32[12,32,128]{2,0,1:T(8,128)S(1)}, u32[]{:S(2)}) copy-start(f32[12,32,128]{2,0,1:T(8,128)S(1)} %get-tuple-element.53) | copy-start | bytes 589828
  27.5 2.1 %copy-start.22 = (f32[12,32,128]{2,0,1:T(8,128)}, f32[12,32,128]{2,0,1:T(8,128)S(1)}, u32[]{:S(2)}) copy-start(f32[12,32,128]{2,0,1:T(8,128)S(1)} %get-tuple-element.25) | copy-start | bytes 589828
  27.5 2.1 %copy-start.25 = (f32[12,32,128]{2,0,1:T(8,128)}, f32[12,32,128]{2,0,1:T(8,128)S(1)}, u32[]{:S(2)}) copy-start(f32[12,32,128]{2,0,1:T(8,128)S(1)} %get-tuple-element.26) | copy-start | bytes 589828
  27.5 2.1 %copy-start.28 = (f32[12,32,128]{2,0,1:T(8,128)}, f32[12,32,128]{2,0,1:T(8,128)S(1)}, u32[]{:S(2)}) copy-start(f32[12,32,128]{2,0,1:T(8,128)S(1)} %get-tuple-element.27) | copy-start | bytes 589828
  30.4 11.1 %copy-start.19 = (bf16[16,32,196]{2,1,0:T(8,128)(2,1)}, bf16[16,32,196]{2,1,0:T(8,128)(2,1)S(1)}, u32[]{:S(2)}) copy-start(bf16[16,32,196]{2,1,0:T(8,128)(2,1)S(1)} %all-to-all-done) | copy-start | bytes 602116
  30.5 8.0 %collective-permute-start = (bf16[512,196]{0,1:T(8,128)(2,1)S(1)}, bf16[512,196]{0,1:T(8,128)(2,1)S(1)}, u32[]{:S(2)}, u32[]{:S(2)}) collective-permute-start(bf16[512,196]{0,1:T(8,128)(2,1)S(1)} %copy.35), channel_id=1, source_target_pairs={{0,1},{1,2},{2,3},{3,4},{4,5},{5,6},{6,7},{7,8},{8,9},{9,10},{10,1... | collective-permute-start | bytes 602120 | tf_op jit(solution)/shard_map/ppermute | solution.py:16
  31.0 7.6 %collective-permute-start.1 = (bf16[512,196]{0,1:T(8,128)(2,1)S(1)}, bf16[512,196]{0,1:T(8,128)(2,1)S(1)}, u32[]{:S(2)}, u32[]{:S(2)}) collective-permute-start(bf16[512,196]{0,1:T(8,128)(2,1)S(1)} %copy.35), channel_id=1, source_target_pairs={{1,0},{2,1},{3,2},{4,3},{5,4},{6,5},{7,6},{8,7},{9,8},{10,9},{11,1... | collective-permute-start | bytes 602120 | tf_op jit(solution)/shard_map/ppermute | solution.py:16
  35.8 5.7 %copy-start.37 = (bf16[1,512,196]{1,2,0:T(8,128)(2,1)}, bf16[1,512,196]{1,2,0:T(8,128)(2,1)S(1)}, u32[]{:S(2)}) copy-start(bf16[1,512,196]{1,2,0:T(8,128)(2,1)S(1)} %copy.37) | copy-start | bytes 602116
  43.2 1.3 copy-start.4
  46.6 1.1 copy-start.29
  57.7 1.7 %copy-start.45 = (f32[5,32,128]{2,0,1:T(8,128)S(1)}, f32[5,32,128]{2,0,1:T(8,128)}, u32[]{:S(2)}) copy-start(f32[5,32,128]{2,0,1:T(8,128)} %fusion.186) | copy-start | bytes 245764
  58.5 3.9 %copy-start.55 = (pred[3,512,512]{1,2,0:T(32,128)(4,1)}, pred[3,512,512]{1,2,0:T(32,128)(4,1)S(1)}, u32[]{:S(2)}) copy-start(pred[3,512,512]{1,2,0:T(32,128)(4,1)S(1)} %iota_compare_fusion) | copy-start | bytes 2359300
  62.2 4.1 %copy-start.17 = (f32[6,4,32,128]{3,1,2,0:T(4,128)}, f32[6,4,32,128]{3,1,2,0:T(4,128)S(1)}, u32[]{:S(2)}) copy-start(f32[6,4,32,128]{3,1,2,0:T(4,128)S(1)} %fusion.117) | copy-start | bytes 1179652
  62.2 22.8 %copy-start.38 = (bf16[1,512,196]{1,2,0:T(8,128)(2,1)S(1)}, bf16[1,512,196]{1,2,0:T(8,128)(2,1)}, u32[]{:S(2)}) copy-start(bf16[1,512,196]{1,2,0:T(8,128)(2,1)} %copy-done.37) | copy-start | bytes 602116
  62.2 22.8 %copy-start.52 = (bf16[512,196]{0,1:T(8,128)(2,1)S(1)}, bf16[512,196]{0,1:T(8,128)(2,1)}, u32[]{:S(2)}) copy-start(bf16[512,196]{0,1:T(8,128)(2,1)} %copy-done.51) | copy-start | bytes 602116
  62.2 22.8 %copy-start.54 = (bf16[512,196]{0,1:T(8,128)(2,1)S(1)}, bf16[512,196]{0,1:T(8,128)(2,1)}, u32[]{:S(2)}) copy-start(bf16[512,196]{0,1:T(8,128)(2,1)} %copy-done.53) | copy-start | bytes 602116
  66.4 12.3 %all-to-all-start.1 = ((f32[16,1,514]{2,1,0:T(1,128)}), f32[16,1,514]{2,1,0:T(1,128)S(1)}, u32[]{:S(2)}, u32[]{:S(2)}) async-start(f32[16,1,514]{2,1,0:T(1,128)} %broadcast_in_dim.66), calls=%async_computation.1 | async-start | bytes 81920 | tf_op jit(solution)/shard_map/all_to_all | solution.py:159
  101.9 3.8 %copy-start.42 = (f32[8,32,128]{2,0,1:T(8,128)S(1)}, f32[8,32,128]{2,0,1:T(8,128)}, u32[]{:S(2)}) copy-start(f32[8,32,128]{2,0,1:T(8,128)} %slice_bitcast_fusion.10) | copy-start | bytes 393220
  107.1 1.4 %copy-start.2 = (f32[6,9,32,128]{3,1,2,0:T(8,128)S(1)}, f32[6,9,32,128]{3,1,2,0:T(8,128)}, u32[]{:S(2)}) copy-start(f32[6,9,32,128]{3,1,2,0:T(8,128)} %fusion.46) | copy-start | bytes 2654212
  116.7 20.0 %copy-start.18 = (f32[6,4,32,128]{3,1,2,0:T(4,128)S(1)}, f32[6,4,32,128]{3,1,2,0:T(4,128)}, u32[]{:S(2)}) copy-start(f32[6,4,32,128]{3,1,2,0:T(4,128)} %copy-done.17) | copy-start | bytes 1179652
  117.4 21.5 %copy-start.1 = (bf16[64,192]{1,0:T(8,128)(2,1)S(1)}, bf16[64,192]{1,0:T(8,128)(2,1)}, u32[]{:S(2)}) copy-start(bf16[64,192]{1,0:T(8,128)(2,1)} %param.14) | copy-start | bytes 73732
  119.0 19.3 %copy-start.74 = (bf16[256]{0:T(256)(128)(2,1)S(1)}, bf16[256]{0:T(256)(128)(2,1)}, u32[]{:S(2)}) copy-start(bf16[256]{0:T(256)(128)(2,1)} %param.9) | copy-start | bytes 1540
  (49 other events, 46.2 us)
where the time goes:
time: 140 us; the launch traced here: 139 us
  local copies, waits for them, and re-layouts  52.2 us (37%)
  other arithmetic  32 us (23%)
  starting transfers between devices  19.3 us (14%)
  waiting for transfers between devices  9.05 us (6%)
  blocking collectives  8.97 us (6%)
  between operations  8.92 us (6%)
  matrix products  8.45 us (6%)
    unnamed x153, local copies, waits for them, and re-layouts  16.7 us
    ppermute x4, starting transfers between devices, neighbours(): return (lax.ppermute(block, axis, up), lax.ppermute(block, axis, down))  10.1 us
    all_to_all x1, blocking collectives, on_device(): lax.all_to_all(message, 'lon', split_axis=0, concat_axis=0, tiled=True)  8.97 us
    all_to_all x1, waiting for transfers between devices, on_device(): lax.all_to_all(message, 'lon', split_axis=0, concat_axis=0, tiled=True)  6.54 us
    gather x12, local copies, waits for them, and re-layouts  6.29 us
    slice x10, local copies, waits for them, and re-layouts, solve_vertical(): alpha, gamma = (alpha[first:first + count], gamma[first:first + count])  6.19 us
    all_to_all x1, starting transfers between devices, on_device(): lax.all_to_all(message, 'lon', split_axis=0, concat_axis=0, tiled=True)  5.63 us
    add x16, other arithmetic, solve_vertical(): field + alpha * shifted(field, stride, 0.0)  4.96 us
  transfers between devices with their start and end apart: 6, of which 2 were waited for; matrix products, arithmetic and copies ran while one was open for 14% of the time, Pallas kernels for 0%

commit v1 on v0

v1 whole, which is shorter than its diff:
```python
import jax
import jax.numpy as jnp
from jax import lax
from jax.experimental import pallas as pl
from jax.experimental.pallas import tpu as pltpu
from jax.sharding import PartitionSpec as P

VARS = 6
LEV = 32
STEPS = 2
EXACT = lax.Precision.HIGHEST


def neighbours(block, axis):
    count = lax.axis_size(axis)
    up = [(i, (i + 1) % count) for i in range(count)]
    down = [(target, source) for source, target in up]
    return lax.ppermute(block, axis, up), lax.ppermute(block, axis, down)


def factor_vertical(vert):
    levels = vert.shape[-2]
    level = lax.broadcasted_iota(jnp.int32, vert.shape, vert.ndim - 2)
    axis = vert.ndim - 2
    upward = jnp.where(level < levels - 1, vert, 0.0)
    downward = jnp.where(level > 0, pltpu.roll(upward, 1, axis), 0.0)
    lower, upper = -downward, -upward
    diag = 1.0 + downward + upward
    factors = []
    stride = 1
    while stride < levels:
        back = levels - stride
        alpha = -lower / pltpu.roll(diag, stride, axis)
        gamma = -upper / pltpu.roll(diag, back, axis)
        new_lower = alpha * pltpu.roll(lower, stride, axis)
        new_upper = gamma * pltpu.roll(upper, back, axis)
        diag = diag + alpha * pltpu.roll(upper, stride, axis) + gamma * pltpu.roll(lower, back, axis)
        factors.append((alpha, gamma))
        lower, upper = new_lower, new_upper
        stride *= 2
    return factors, 1.0 / diag


def solve_vertical(alphas, gammas, scale, field, first):
    count, levels = field.shape[:2]
    held = pl.ds(first, count)
    for step in range(alphas.shape[0]):
        stride = 2**step
        field = (
            field
            + alphas[step, held] * pltpu.roll(field, stride, 1)
            + gammas[step, held] * pltpu.roll(field, levels - stride, 1)
        )
    return field * scale[held]


def smooth(along, across, field, first):
    nlat = field.shape[-1]
    for _ in range(STEPS):
        count = field.shape[0]
        flux_lon = along[pl.ds(first, count - 1)] * (field[1:] - field[:-1])
        middle = field[1:-1]
        flux_lat = across[pl.ds(first + 1, count - 2)] * (pltpu.roll(middle, nlat - 1, 2) - middle)
        field = middle + flux_lon[1:] - flux_lon[:-1] + flux_lat - pltpu.roll(flux_lat, 1, 2)
        first += 1
    return field


def thirds(value):
    parts = []
    for _ in range(3):
        part = value.astype(jnp.bfloat16)
        parts.append(part)
        value = value - part.astype(jnp.float32)
    return parts


def matmul(left, right, contract):
    return lax.dot_general(
        left, right, (contract, ((), ())), preferred_element_type=jnp.float32
    )


def hit_matrix(column, percol):
    cell = lax.broadcasted_iota(jnp.int32, (percol, column.shape[1]), 0).astype(jnp.float32)
    return jnp.where(cell == column, 1.0, 0.0).astype(jnp.bfloat16)


def adjoint(weights, hits, values, block):
    spread = weights[block].astype(jnp.float32) * values
    return sum(matmul(part, hits[block], ((1,), (1,))) for part in thirds(spread))


def forward(weights, hits, field):
    flat = jnp.concatenate([field[x] for x in range(field.shape[0])], axis=1)
    picked = sum(matmul(part, hits[1], ((1,), (0,))) for part in thirds(flat))
    return jnp.sum(weights[1].astype(jnp.float32) * picked, axis=0, keepdims=True)


def spread_out(values, weights, hits, field, width):
    for block in range(3):
        flat = adjoint(weights, hits, values[block], block)
        lanes = flat.shape[1] // width
        for x in range(width):
            field[block * width + x] = flat[:, x * lanes : (x + 1) * lanes]


def total(value, lanes):
    return jnp.full((1, lanes), jnp.sum(value), jnp.float32)


def first_kernel(
    coeffs_low, coeffs, coeffs_high, left, mine, right,
    rhs, root, weights, hits, along, across, alphas, gammas, scale, precision, message,
    field, norm,
):
    width, levels, nlat = coeffs.shape[1:]
    depth = weights.shape[1]
    for place, source in enumerate((coeffs_low, coeffs, coeffs_high)):
        held = pl.ds(place * width, width)
        along[held] = source[0]
        across[held] = source[1]
        factors, inverse = factor_vertical(source[2])
        scale[held] = inverse
        for step, (alpha, gamma) in enumerate(factors):
            alphas[step, held] = alpha
            gammas[step, held] = gamma
    start = []
    for block, source in enumerate((left, mine, right)):
        turned = source[...].astype(jnp.float32).T
        weights[block] = turned[:depth].astype(jnp.bfloat16)
        column = turned[depth + 2 : depth + 3] * 16.0 + turned[depth + 3 : depth + 4]
        hits[block] = hit_matrix(column, width * nlat)
        start.append(turned[depth : depth + 1] * turned[depth + 1 : depth + 2])
        if block == 1:
            precision[...] = turned[depth : depth + 1]
    spread_out(start, weights, hits, field, width)
    norm[...] = jnp.zeros_like(norm)

    def variable(index, carry):
        part = pl.ds(pl.multiple_of(index * levels, levels), levels)
        solved = solve_vertical(alphas, gammas, scale, field[:, part, :], 0)
        own = smooth(along, across, solved, 0)
        rhs[:, part, :] = own
        inner = own[STEPS : STEPS + width]
        norm[...] += jnp.sum(inner * inner, axis=0)
        root[:, part, :] = solve_vertical(
            alphas, gammas, scale, smooth(along, across, own, STEPS), width
        )
        return carry

    lax.fori_loop(0, VARS, variable, 0)
    seen = forward(weights, hits, root)
    weighted = precision[...] * seen
    slots = seen.shape[1]
    message[0:1, :] = weighted
    message[1:2, :] = seen
    message[2:3, :] = total(norm[...], slots)
    message[3:4, :] = total(weighted * seen, slots)
    message[4:8, :] = jnp.zeros((4, slots), jnp.float32)


def second_kernel(
    around, gathered, message, rhs, weights, hits, along, across, alphas, gammas, scale, precision,
    residual, root, sent,
    field, norm, cross,
):
    levels, nlat = scale.shape[1:]
    width = residual.shape[0]
    slots = precision.shape[1]
    values = [gathered[pl.ds(around[block], 1), 0:slots] for block in range(3)]
    spread_out(values, weights, hits, field, width)
    first = jnp.sum(gathered[:, slots : slots + nlat], axis=0, keepdims=True)
    fit = jnp.sum(gathered[:, slots + nlat : slots + 2 * nlat], axis=0, keepdims=True)
    alpha = (first / (first + fit))[None]
    norm[...] = jnp.zeros_like(norm)
    cross[...] = jnp.zeros_like(cross)

    def variable(index, carry):
        part = pl.ds(pl.multiple_of(index * levels, levels), levels)
        solved = solve_vertical(alphas, gammas, scale, field[:, part, :], 0)
        start = rhs[:, part, :]
        image = start + smooth(along, across, solved, 0)
        left = start - alpha * image
        inner = left[STEPS : STEPS + width]
        residual[:, part, :] = inner
        norm[...] += jnp.sum(inner * inner, axis=0)
        cross[...] += jnp.sum(inner * start[STEPS : STEPS + width], axis=0)
        root[:, part, :] = solve_vertical(
            alphas, gammas, scale, smooth(along, across, left, STEPS), width
        )
        return carry

    lax.fori_loop(0, VARS, variable, 0)
    seen = forward(weights, hits, root)
    weighted = precision[...] * seen
    sent[0:1, :] = seen
    sent[1:2, :] = total(norm[...], slots)
    sent[2:3, :] = total(cross[...], slots)
    sent[3:4, :] = total(weighted * seen, slots)
    sent[4:5, :] = total(weighted * message[1:2, :], slots)
    sent[5:8, :] = jnp.zeros((3, slots), jnp.float32)


def on_device(
    obs_departure,
    obs_precision,
    obs_columns,
    obs_counts,
    obs_blocks,
    weight_table,
    lon_coeff,
    lat_coeff,
    vert_coeff,
):
    devices = lax.axis_size("lon")
    me = lax.axis_index("lon")
    levels, width, nlat = lon_coeff.shape
    percol = width * nlat
    depth = VARS * LEV
    per_dev = obs_columns.shape[0]
    capacity = max(per_dev // 64, 2 * ((per_dev + devices - 1) // devices))
    slots_all = devices * capacity
    bf16, f32 = jnp.bfloat16, jnp.float32

    open_face = jnp.arange(nlat) < nlat - 1
    coeffs = jnp.stack([lon_coeff, jnp.where(open_face, lat_coeff, 0.0), vert_coeff])
    coeffs = coeffs.transpose(0, 2, 1, 3)
    below, above = neighbours(coeffs, "lon")

    slot = jnp.arange(per_dev, dtype=jnp.int32)
    live = slot < obs_counts[0]
    owner = obs_columns // percol
    local_col = obs_columns - owner * percol
    hits = (owner[:, None] == jnp.arange(devices, dtype=jnp.int32)) & live[:, None]
    before = jnp.dot(
        (slot[:, None] > slot).astype(bf16), hits.astype(bf16), preferred_element_type=f32
    )
    rank = jnp.sum(jnp.where(hits, before, 0.0), axis=1).astype(jnp.int32)
    target = jnp.where(live, owner * capacity + rank, slots_all)
    place = jnp.arange(slots_all, dtype=jnp.int32)[:, None] == target
    rows = weight_table.shape[0]
    pick = (obs_blocks[:, None] == jnp.arange(rows, dtype=jnp.int32)).astype(bf16)
    block_rows = jnp.dot(pick, weight_table, preferred_element_type=f32).astype(bf16)
    extra = jnp.stack(
        [
            obs_precision,
            obs_departure,
            (local_col // 16).astype(bf16),
            (local_col % 16).astype(bf16),
        ],
        axis=1,
    )
    lanes = -(-(depth + 4) // 128) * 128
    payload = jnp.concatenate([block_rows, extra], axis=1)
    payload = jnp.pad(payload, ((0, 0), (0, lanes - depth - 4)))
    payload = jnp.dot(place.astype(bf16), payload, preferred_element_type=f32).astype(bf16)
    mine = lax.all_to_all(payload, "lon", split_axis=0, concat_axis=0, tiled=True)
    left, right = neighbours(mine, "lon")
    wide = 3 * width
    middle = width + 2 * STEPS
    steps = (levels - 1).bit_length()
    vmem = pl.BlockSpec(memory_space=pltpu.VMEM)
    limit = pltpu.CompilerParams(vmem_limit_bytes=40 * 2**20)

    def shape(*dims, dtype=f32):
        return jax.ShapeDtypeStruct(dims, dtype)

    rhs, rhs_root, *held, message = pl.pallas_call(
        first_kernel,
        out_shape=[
            shape(middle, depth, nlat),
            shape(width, depth, nlat),
            shape(3, depth, slots_all, dtype=bf16),
            shape(3, percol, slots_all, dtype=bf16),
            shape(wide, levels, nlat),
            shape(wide, levels, nlat),
            shape(steps, wide, levels, nlat),
            shape(steps, wide, levels, nlat),
            shape(wide, levels, nlat),
            shape(1, slots_all),
            shape(8, slots_all),
        ],
        in_specs=[vmem] * 6,
        out_specs=[vmem] * 11,
        scratch_shapes=[pltpu.VMEM((wide, depth, nlat), f32), pltpu.VMEM((levels, nlat), f32)],
        compiler_params=limit,
    )(below, coeffs, above, left, mine, right)
    rhs_obs = message[1]
    gathered = jnp.concatenate([message[0], message[2, :nlat], message[3, :nlat]])
    gathered = jnp.broadcast_to(gathered, (devices, slots_all + 2 * nlat))
    gathered = lax.all_to_all(gathered, "lon", split_axis=0, concat_axis=0, tiled=True)
    norm = jnp.sum(gathered[:, slots_all])
    fit_norm = jnp.sum(gathered[:, slots_all + nlat])
    around = jnp.stack([(me + devices - 1) % devices, me, (me + 1) % devices])
    residual, residual_root, sent = pl.pallas_call(
        second_kernel,
        out_shape=[
            shape(width, depth, nlat),
            shape(width, depth, nlat),
            shape(8, slots_all),
        ],
        in_specs=[pl.BlockSpec(memory_space=pltpu.SMEM)] + [vmem] * 11,
        out_specs=[vmem] * 3,
        scratch_shapes=[pltpu.VMEM((wide, depth, nlat), f32)]
        + [pltpu.VMEM((levels, nlat), f32)] * 2,
        compiler_params=limit,
    )(around, gathered, message, rhs, *held)
    message = jnp.concatenate(
        [
            rhs_obs.reshape(devices, capacity),
            sent[0].reshape(devices, capacity),
            jnp.broadcast_to(sent[1:5, 0], (devices, 4)),
        ],
        axis=1,
    )
    message = lax.all_to_all(message, "lon", split_axis=0, concat_axis=0, tiled=True)
    fresh, cross, fit_fresh, fit_cross = jnp.sum(message[:, 2 * capacity :], axis=0)
    alpha = norm / (norm + fit_norm)
    beta = fresh / norm
    curve = (
        fresh + fit_fresh + 2.0 * beta * (cross + fit_cross) + beta * beta * (norm + fit_norm)
    )
    second = fresh / curve
    first = alpha + second * beta
    control = first * rhs[STEPS : STEPS + width] + second * residual
    increment = first * rhs_root + second * residual_root
    fit = first * message[:, :capacity] + second * message[:, capacity : 2 * capacity]
    fit = jnp.dot(fit.reshape(1, slots_all), place.astype(f32), precision=EXACT)[0]
    obs_fit = jnp.where(live, fit - obs_departure.astype(f32), 0.0)


    def placed(field):
        return field.reshape(width, VARS, levels, nlat).transpose(1, 2, 0, 3)

    return placed(control), placed(increment), obs_fit


def solution(mesh):
    in_specs = (
        P(("member", "lon")),
        P("lon"),
        P("lon"),
        P("lon"),
        P("lon"),
        P("lon", None),
        P(None, "lon", None),
        P(None, "lon", None),
        P(None, "lon", None),
    )
    out_specs = (
        P("member", None, "lon", None),
        P("member", None, "lon", None),
        P(("member", "lon")),
    )
    return jax.shard_map(
        on_device, mesh=mesh, in_specs=in_specs, out_specs=out_specs, check_vma=False
    )
```

time: 140 us -> 102 us (0.73)
  local copies, waits for them, and re-layouts: 52.2 us -> 23.9 us
  other arithmetic: 32 us -> 5.61 us
  Pallas kernels: 0 us -> 14.2 us
  waiting for transfers between devices: 9.05 us -> 22.1 us
  blocking collectives: 8.97 us -> 0 us
  matrix products: 8.45 us -> 2.34 us
  starting transfers between devices: 19.3 us -> 24.8 us
    pallas_call x0 -> x2, Pallas kernels: none -> 14.2 us  [the longest x1 7.14 us: on_device(): pl.pallas_call(second_kernel, out_shape=[shape(width, depth, nlat), shape...]
    slice x35 -> x3, local copies, waits for them, and re-layouts: 13.6 us -> 0.15 us  [the longest x1 0.11 us: on_device(): sent[1:5, 0]]
    mul x26 -> x0, other arithmetic: 9.08 us -> none  [the longest x8 4.66 us: smooth(): across[first + 1:first + count - 1] * (jnp.roll(middle, -1, -1) - middle)]
    all_to_all x1 -> x0, blocking collectives: 8.97 us -> none  [on_device(): lax.all_to_all(message, 'lon', split_axis=0, concat_axis=0, tiled=True)]
    all_to_all x1, waiting for transfers between devices: 0.01 us -> 8.3 us  [on_device(): lax.all_to_all(payload, 'lon', split_axis=0, concat_axis=0, tiled=True)]
    dot_general x4 -> x0, matrix products: 6.8 us -> none  [the longest x2 4.37 us: adjoint(): flat = jnp.einsum('bsc,bsn->cbn', weights, spread, precision=EXACT)]
    all_to_all x0 -> x1, waiting for transfers between devices: none -> 6.61 us  [on_device(): lax.all_to_all(gathered, 'lon', split_axis=0, concat_axis=0, tiled=True)]
    gather x12 -> x0, local copies, waits for them, and re-layouts: 6.29 us -> none
  transfers between devices with their start and end apart: 6 -> 7, of which waited for: 2 -> 4; matrix products, arithmetic and copies ran while one was open for 14% -> 3% of each run, Pallas kernels for 0% -> 0%
where the time goes in v1:
time: 102 us; the launch traced here: 101 us
  starting transfers between devices  24.8 us (24%)
  local copies, waits for them, and re-layouts  23.9 us (23%)
  waiting for transfers between devices  22.1 us (22%)
  Pallas kernels  14.2 us (14%)
  between operations  7.84 us (8%)
  other arithmetic  5.61 us (6%)
  matrix products  2.34 us (2%)
    unnamed x52, local copies, waits for them, and re-layouts  18.7 us
    ppermute x4, starting transfers between devices, neighbours(): return (lax.ppermute(block, axis, up), lax.ppermute(block, axis, down))  8.93 us
    all_to_all x1, waiting for transfers between devices, on_device(): lax.all_to_all(payload, 'lon', split_axis=0, concat_axis=0, tiled=True)  8.3 us
    all_to_all x1, starting transfers between devices, on_device(): lax.all_to_all(payload, 'lon', split_axis=0, concat_axis=0, tiled=True)  7.38 us
    pallas_call x1, Pallas kernels, on_device(): pl.pallas_call(second_kernel, out_shape=[shape(width, depth, nlat), shape...  7.14 us
    pallas_call x1, Pallas kernels, on_device(): pl.pallas_call(first_kernel, out_shape=[shape(middle, depth, nlat), shape...  7.04 us
    all_to_all x1, waiting for transfers between devices, on_device(): lax.all_to_all(gathered, 'lon', split_axis=0, concat_axis=0, tiled=True)  6.61 us
    all_to_all x1, starting transfers between devices, on_device(): lax.all_to_all(gathered, 'lon', split_axis=0, concat_axis=0, tiled=True)  5.05 us
  transfers between devices with their start and end apart: 7, of which 4 were waited for; matrix products, arithmetic and copies ran while one was open for 3% of the time, Pallas kernels for 0%

profile of v1, /device:TPU:0, one launch (start us, length us, event | category | flops | bytes accessed | tf_op | source)
XLA Modules:
  0.0 100.7 jit_solution(7167112595615648635)
XLA Ops:
  4.3 1.0 convolution_convert_fusion.1
  5.3 1.0 convolution_convert_fusion
  6.2 7.4 %all-to-all-start = ((bf16[16,32,256]{2,1,0:T(8,128)(2,1)}), bf16[16,32,256]{2,1,0:T(8,128)(2,1)S(1)}, u32[]{:S(2)}, u32[]{:S(2)}) async-start(bf16[16,32,256]{2,1,0:T(8,128)(2,1)} %bitcast.5), calls=%async_computation | async-start | bytes 524288 | tf_op jit(solution)/shard_map/all_to_all | solution.py:258
  13.6 0.8 copy.42
  14.5 0.9 copy_bitcast_fusion.2
  15.4 8.3 %all-to-all-done = bf16[16,32,256]{2,1,0:T(8,128)(2,1)S(1)} async-done(((bf16[16,32,256]{2,1,0:T(8,128)(2,1)}), bf16[16,32,256]{2,1,0:T(8,128)(2,1)S(1)}, u32[]{:S(2)}, u32[]{:S(2)}) %all-to-all-start) | async-done | bytes 262176 | tf_op jit(solution)/shard_map/all_to_all | solution.py:258
  23.7 4.4 %collective-permute-start.3 = (bf16[512,256]{1,0:T(8,128)(2,1)S(1)}, bf16[512,256]{1,0:T(8,128)(2,1)S(1)}, u32[]{:S(2)}, u32[]{:S(2)}) collective-permute-start(bf16[512,256]{1,0:T(8,128)(2,1)S(1)} %bitcast.43), channel_id=1, source_target_pairs={{1,0},{2,1},{3,2},{4,3},{5,4},{6,5},{7,6},{8,7},{9,8},{10,9},{11,1... | collective-permute-start | bytes 786440 | tf_op jit(solution)/shard_map/ppermute | solution.py:18
  28.2 4.4 %collective-permute-start.1 = (f32[3,4,32,128]{3,2,1,0:T(8,128)S(1)}, f32[3,4,32,128]{3,2,1,0:T(8,128)S(1)}, u32[]{:S(2)}, u32[]{:S(2)}) collective-permute-start(f32[3,4,32,128]{3,2,1,0:T(8,128)S(1)} %maximum_bitcast_fusion.coeffs), channel_id=1, source_target_pairs={{1,0},{2,1},{3,2},{4,3},{5,4},{6,5},{7,6},{8,7},{9,8},{10,9},{11,1... | collective-permute-start | bytes 589832 | tf_op jit(solution)/shard_map/ppermute | solution.py:18
  32.6 3.5 %collective-permute-done.coeffs_low = f32[3,4,32,128]{3,2,1,0:T(8,128)S(1)} collective-permute-done((f32[3,4,32,128]{3,2,1,0:T(8,128)S(1)}, f32[3,4,32,128]{3,2,1,0:T(8,128)S(1)}, u32[]{:S(2)}, u32[]{:S(2)}) %collective-permute-start) | collective-permute-done | bytes 196640 | tf_op jit(solution)/shard_map/ppermute | solution.py:18
  38.8 0.9 copy-done.11
  39.8 0.9 copy-done.13
  40.7 0.9 copy-done.15
  41.7 0.9 copy-done.17
  42.6 7.0 %shard_map.112 = (f32[8,192,128]{2,1,0:T(8,128)S(1)}, f32[4,192,128]{2,1,0:T(8,128)S(1)}, bf16[3,192,512]{2,1,0:T(8,128)(2,1)S(1)}, bf16[3,512,512]{2,1,0:T(8,12...) custom-call(f32[3,4,32,128]{3,2,1,0:T(8,128)S(1)} %copy-done.15, ...), custom_call_target="tpu_custom_call" | custom-call | tf_op jit(solution)/shard_map/pallas_call | solution.py:269
  49.6 0.9 copy-done.1
  50.6 1.0 copy-done.3
  51.6 0.7 copy-done.5
  55.0 5.0 %all-to-all-start.1 = ((f32[16,1,768]{2,1,0:T(1,128)}), f32[16,1,768]{2,1,0:T(1,128)S(1)}, u32[]{:S(2)}, u32[]{:S(2)}) async-start(f32[16,1,768]{2,1,0:T(1,128)} %broadcast_in_dim.36), calls=%async_computation.1 | async-start | bytes 98304 | tf_op jit(solution)/shard_map/all_to_all | solution.py:292
  60.2 6.6 %all-to-all-done.1 = f32[16,1,768]{2,1,0:T(1,128)S(1)} async-done(((f32[16,1,768]{2,1,0:T(1,128)}), f32[16,1,768]{2,1,0:T(1,128)S(1)}, u32[]{:S(2)}, u32[]{:S(2)}) %all-to-all-start.1) | async-done | bytes 49184 | tf_op jit(solution)/shard_map/all_to_all | solution.py:292
  66.8 1.2 %copy-done.2 = f32[5,12,32,128]{3,2,1,0:T(8,128)S(1)} copy-done((f32[5,12,32,128]{3,2,1,0:T(8,128)S(1)}, f32[5,12,32,128]{3,2,1,0:T(8,128)}, u32[]{:S(2)}) %copy-start.2) | copy-done | bytes 983064
  68.0 1.2 %copy-done.4 = f32[5,12,32,128]{3,2,1,0:T(8,128)S(1)} copy-done((f32[5,12,32,128]{3,2,1,0:T(8,128)S(1)}, f32[5,12,32,128]{3,2,1,0:T(8,128)}, u32[]{:S(2)}) %copy-start.4) | copy-done | bytes 983064
  69.2 0.9 copy-done.19
  70.2 0.9 copy-done.21
  71.1 0.9 copy-done.23
  72.0 7.1 %shard_map.113 = (f32[4,192,128]{2,1,0:T(8,128)S(1)}, f32[4,192,128]{2,1,0:T(8,128)S(1)}, f32[8,512]{1,0:T(8,128)S(1)}) custom-call(s32[3]{0:T(128)S(1)} %pad_add_fusion.around, f32[16,768]{1,0:T(8,128)S(1)} %bitcast.45, f32[8,512]{1,0:T(8,128)S(1)} %get-tuple-element.17.message, f32[8,192,128]{2,1,0:T(8,128)S(1)} %get-tuple-element.18.rhs, ...), custom_call_target="tpu_custom_call" | custom-call | tf_op jit(solution)/shard_map/pallas_call | solution.py:296
  79.2 0.7 copy-done.7
  79.9 0.7 copy-done.9
  81.6 3.5 %all-to-all-start.2 = ((f32[16,1,68]{2,1,0:T(1,128)}), f32[16,1,68]{2,1,0:T(1,128)S(1)}, u32[]{:S(2)}, u32[]{:S(2)}) async-start(f32[16,1,68]{2,1,0:T(1,128)} %bitcast.13), calls=%async_computation.2 | async-start | bytes 16384 | tf_op jit(solution)/shard_map/all_to_all | solution.py:317
  87.8 3.7 %all-to-all-done.2 = f32[16,1,68]{2,1,0:T(1,128)S(1)} async-done(((f32[16,1,68]{2,1,0:T(1,128)}), f32[16,1,68]{2,1,0:T(1,128)S(1)}, u32[]{:S(2)}, u32[]{:S(2)}) %all-to-all-start.2) | async-done | bytes 4384 | tf_op jit(solution)/shard_map/all_to_all | solution.py:317
  97.0 1.1 %multiply_add_fusion = f32[4,192,128]{2,1,0:T(8,128)S(1)} fusion(f32[4,192,128]{2,1,0:T(8,128)} %copy-done.9, f32[4,192,128]{2,1,0:T(8,128)S(1)} %copy-done.6, f32[]{:T(128)S(6)} %div.41, f32[]{:T(128)S(6)} %add.69), kind=kLoop, calls=%fused_computation.8 | loop fusion | flops 294912 | bytes 1179656 | tf_op jit(solution)/shard_map/add | solution.py:327
  98.1 1.0 copy.40
  99.2 1.0 copy.41
  (72 shorter events, 12.1 us)
Async XLA Ops:
  0.6 3.6 %copy-start = (bf16[64,192]{1,0:T(8,128)(2,1)S(1)}, bf16[64,192]{1,0:T(8,128)(2,1)}, u32[]{:S(2)}) copy-start(bf16[64,192]{1,0:T(8,128)(2,1)} %param.14) | copy-start | bytes 73732
  6.2 17.4 %all-to-all-start = ((bf16[16,32,256]{2,1,0:T(8,128)(2,1)}), bf16[16,32,256]{2,1,0:T(8,128)(2,1)S(1)}, u32[]{:S(2)}, u32[]{:S(2)}) async-start(bf16[16,32,256]{2,1,0:T(8,128)(2,1)} %bitcast.5), calls=%async_computation | async-start | bytes 524288 | tf_op jit(solution)/shard_map/all_to_all | solution.py:258
  23.7 13.8 %collective-permute-start.2 = (bf16[512,256]{1,0:T(8,128)(2,1)S(1)}, bf16[512,256]{1,0:T(8,128)(2,1)S(1)}, u32[]{:S(2)}, u32[]{:S(2)}) collective-permute-start(bf16[512,256]{1,0:T(8,128)(2,1)S(1)} %bitcast.42), channel_id=1, source_target_pairs={{0,1},{1,2},{2,3},{3,4},{4,5},{5,6},{6,7},{7,8},{8,9},{9,10},{10,1... | collective-permute-start | bytes 786440 | tf_op jit(solution)/shard_map/ppermute | solution.py:18
  23.7 14.5 %collective-permute-start.3 = (bf16[512,256]{1,0:T(8,128)(2,1)S(1)}, bf16[512,256]{1,0:T(8,128)(2,1)S(1)}, u32[]{:S(2)}, u32[]{:S(2)}) collective-permute-start(bf16[512,256]{1,0:T(8,128)(2,1)S(1)} %bitcast.43), channel_id=1, source_target_pairs={{1,0},{2,1},{3,2},{4,3},{5,4},{6,5},{7,6},{8,7},{9,8},{10,9},{11,1... | collective-permute-start | bytes 786440 | tf_op jit(solution)/shard_map/ppermute | solution.py:18
  28.1 8.0 %collective-permute-start = (f32[3,4,32,128]{3,2,1,0:T(8,128)S(1)}, f32[3,4,32,128]{3,2,1,0:T(8,128)S(1)}, u32[]{:S(2)}, u32[]{:S(2)}) collective-permute-start(f32[3,4,32,128]{3,2,1,0:T(8,128)S(1)} %maximum_bitcast_fusion.coeffs), channel_id=1, source_target_pairs={{0,1},{1,2},{2,3},{3,4},{4,5},{5,6},{6,7},{7,8},{8,9},{9,10},{10,1... | collective-permute-start | bytes 589832 | tf_op jit(solution)/shard_map/ppermute | solution.py:18
  28.2 8.6 %collective-permute-start.1 = (f32[3,4,32,128]{3,2,1,0:T(8,128)S(1)}, f32[3,4,32,128]{3,2,1,0:T(8,128)S(1)}, u32[]{:S(2)}, u32[]{:S(2)}) collective-permute-start(f32[3,4,32,128]{3,2,1,0:T(8,128)S(1)} %maximum_bitcast_fusion.coeffs), channel_id=1, source_target_pairs={{1,0},{2,1},{3,2},{4,3},{5,4},{6,5},{7,6},{8,7},{9,8},{10,9},{11,1... | collective-permute-start | bytes 589832 | tf_op jit(solution)/shard_map/ppermute | solution.py:18
  36.1 0.7 copy-start.14
  36.7 0.7 copy-start.16
  37.4 0.7 copy-start.10
  38.1 0.7 copy-start.12
  38.8 0.9 copy-start.11
  39.8 0.9 copy-start.13
  40.7 0.9 copy-start.15
  41.7 0.9 copy-start.17
  49.6 1.0 copy-start.1
  50.6 1.0 copy-start.3
  51.6 0.7 copy-start.5
  52.3 0.7 copy-start.18
  53.0 0.7 copy-start.20
  53.7 0.7 copy-start.22
  55.0 11.8 %all-to-all-start.1 = ((f32[16,1,768]{2,1,0:T(1,128)}), f32[16,1,768]{2,1,0:T(1,128)S(1)}, u32[]{:S(2)}, u32[]{:S(2)}) async-start(f32[16,1,768]{2,1,0:T(1,128)} %broadcast_in_dim.36), calls=%async_computation.1 | async-start | bytes 98304 | tf_op jit(solution)/shard_map/all_to_all | solution.py:292
  66.8 1.2 %copy-start.2 = (f32[5,12,32,128]{3,2,1,0:T(8,128)S(1)}, f32[5,12,32,128]{3,2,1,0:T(8,128)}, u32[]{:S(2)}) copy-start(f32[5,12,32,128]{3,2,1,0:T(8,128)} %copy-done.1) | copy-start | bytes 2949124
  68.0 1.2 %copy-start.4 = (f32[5,12,32,128]{3,2,1,0:T(8,128)S(1)}, f32[5,12,32,128]{3,2,1,0:T(8,128)}, u32[]{:S(2)}) copy-start(f32[5,12,32,128]{3,2,1,0:T(8,128)} %copy-done.3) | copy-start | bytes 2949124
  69.2 0.9 copy-start.19
  70.2 0.9 copy-start.21
  71.1 0.9 copy-start.23
  72.0 25.0 %copy-start.6 = (f32[4,192,128]{2,1,0:T(8,128)S(1)}, f32[4,192,128]{2,1,0:T(8,128)}, u32[]{:S(2)}) copy-start(f32[4,192,128]{2,1,0:T(8,128)} %copy-done.5) | copy-start | bytes 1179652
  79.2 0.7 copy-start.7
  79.9 0.7 copy-start.9
  80.7 18.5 %copy-start.8 = (f32[4,192,128]{2,1,0:T(8,128)S(1)}, f32[4,192,128]{2,1,0:T(8,128)}, u32[]{:S(2)}) copy-start(f32[4,192,128]{2,1,0:T(8,128)} %copy-done.7) | copy-start | bytes 1179652
  81.6 9.9 %all-to-all-start.2 = ((f32[16,1,68]{2,1,0:T(1,128)}), f32[16,1,68]{2,1,0:T(1,128)S(1)}, u32[]{:S(2)}, u32[]{:S(2)}) async-start(f32[16,1,68]{2,1,0:T(1,128)} %bitcast.13), calls=%async_computation.2 | async-start | bytes 16384 | tf_op jit(solution)/shard_map/all_to_all | solution.py:317
  98.1 2.1 %copy-start.24 = (bf16[256]{0:T(256)(128)(2,1)S(1)}, bf16[256]{0:T(256)(128)(2,1)}, u32[]{:S(2)}) copy-start(bf16[256]{0:T(256)(128)(2,1)} %param.9) | copy-start | bytes 1540

commit v2 on v1

v2 whole, which is shorter than its diff:
```python
import jax
import jax.numpy as jnp
from jax import lax
from jax.experimental import pallas as pl
from jax.experimental.pallas import tpu as pltpu
from jax.sharding import PartitionSpec as P

VARS = 6
LEV = 32
STEPS = 2
EXACT = lax.Precision.HIGHEST


def factor_vertical(vert):
    levels = vert.shape[-2]
    level = lax.broadcasted_iota(jnp.int32, vert.shape, vert.ndim - 2)
    axis = vert.ndim - 2
    upward = jnp.where(level < levels - 1, vert, 0.0)
    downward = jnp.where(level > 0, pltpu.roll(upward, 1, axis), 0.0)
    lower, upper = -downward, -upward
    diag = 1.0 + downward + upward
    factors = []
    stride = 1
    while stride < levels:
        back = levels - stride
        alpha = -lower / pltpu.roll(diag, stride, axis)
        gamma = -upper / pltpu.roll(diag, back, axis)
        new_lower = alpha * pltpu.roll(lower, stride, axis)
        new_upper = gamma * pltpu.roll(upper, back, axis)
        diag = diag + alpha * pltpu.roll(upper, stride, axis) + gamma * pltpu.roll(lower, back, axis)
        factors.append((alpha, gamma))
        lower, upper = new_lower, new_upper
        stride *= 2
    return factors, 1.0 / diag


def solve_vertical(alphas, gammas, scale, field, first):
    count, levels = field.shape[:2]
    held = pl.ds(first, count)
    for step in range(alphas.shape[0]):
        stride = 2**step
        field = (
            field
            + alphas[step, held] * pltpu.roll(field, stride, 1)
            + gammas[step, held] * pltpu.roll(field, levels - stride, 1)
        )
    return field * scale[held]


def smooth(along, across, field, first):
    nlat = field.shape[-1]
    for _ in range(STEPS):
        count = field.shape[0]
        flux_lon = along[pl.ds(first, count - 1)] * (field[1:] - field[:-1])
        middle = field[1:-1]
        flux_lat = across[pl.ds(first + 1, count - 2)] * (pltpu.roll(middle, nlat - 1, 2) - middle)
        field = middle + flux_lon[1:] - flux_lon[:-1] + flux_lat - pltpu.roll(flux_lat, 1, 2)
        first += 1
    return field


def thirds(value):
    parts = []
    for _ in range(3):
        part = value.astype(jnp.bfloat16)
        parts.append(part)
        value = value - part.astype(jnp.float32)
    return parts


def matmul(left, right, contract):
    return lax.dot_general(
        left, right, (contract, ((), ())), preferred_element_type=jnp.float32
    )


def hit_matrix(column, percol):
    cell = lax.broadcasted_iota(jnp.int32, (percol, column.shape[1]), 0).astype(jnp.float32)
    return jnp.where(cell == column, 1.0, 0.0).astype(jnp.bfloat16)


def adjoint(weights, hits, values, block):
    spread = weights[block].astype(jnp.float32) * values
    return sum(matmul(part, hits[block], ((1,), (1,))) for part in thirds(spread))


def forward(weights, hits, field):
    flat = jnp.concatenate([field[x] for x in range(field.shape[0])], axis=1)
    picked = sum(matmul(part, hits[1], ((1,), (0,))) for part in thirds(flat))
    return jnp.sum(weights[1].astype(jnp.float32) * picked, axis=0, keepdims=True)


def spread_out(values, weights, hits, field, width):
    for block in range(3):
        flat = adjoint(weights, hits, values[block], block)
        lanes = flat.shape[1] // width
        for x in range(width):
            field[block * width + x] = flat[:, x * lanes : (x + 1) * lanes]


def total(value, lanes):
    return jnp.full((1, lanes), jnp.sum(value), jnp.float32)


def whole_kernel(
    coeffs, payload,
    control, increment, last_in,
    coeffs_low, coeffs_high, low, mine, high, weights, hits, along, across, alphas, gammas, scale,
    precision, field, rhs, rhs_root, residual, residual_root, norm, cross,
    z_out, z_low, z_high, sums_out, sums_in, last_out,
    pay_send, pay_recv, relay_send, relay_recv, side_send, side_recv, sums_send, sums_recv,
    last_send, last_recv,
):
    devices = payload.shape[0]
    me = lax.axis_index("lon")
    below, above = lax.rem(me + devices - 1, devices), lax.rem(me + 1, devices)
    width, levels, nlat = coeffs.shape[1:]
    depth = weights.shape[1]
    slots = precision.shape[1]
    rows = slots // nlat

    def remote(source, target, sent, received, device):
        return pltpu.make_async_remote_copy(
            src_ref=source,
            dst_ref=target,
            send_sem=sent,
            recv_sem=received,
            device_id={"lon": device},
            device_id_type=pl.DeviceIdType.MESH,
        )

    def for_peers(act):
        def step(offset, carry):
            act(lax.rem(me + offset, devices))
            return carry

        lax.fori_loop(1, devices, step, 0)

    def to_sides(source, to_above, to_below, slot):
        return (
            remote(source, to_above, side_send.at[slot], side_recv.at[slot], above),
            remote(source, to_below, side_send.at[slot + 1], side_recv.at[slot + 1], below),
        )

    def relay(source, slab):
        return (
            remote(source, low.at[slab], relay_send.at[0, slab], relay_recv.at[0, slab], above),
            remote(source, high.at[slab], relay_send.at[1, slab], relay_recv.at[1, slab], below),
        )

    barrier = pltpu.get_barrier_semaphore()
    for_peers(
        lambda peer: pl.semaphore_signal(
            barrier, inc=1, device_id={"lon": peer}, device_id_type=pl.DeviceIdType.MESH
        )
    )
    pl.semaphore_wait(barrier, devices - 1)

    for_peers(
        lambda peer: remote(
            payload.at[peer], mine.at[me], pay_send.at[peer], pay_recv.at[me], peer
        ).start()
    )
    coeff_copies = to_sides(coeffs, coeffs_low, coeffs_high, 0)
    for copy in coeff_copies:
        copy.start()
    mine[me] = payload[me]
    for copy in relay(mine.at[me], me):
        copy.start()

    def arrival(peer):
        return remote(payload.at[peer], mine.at[peer], pay_send.at[peer], pay_recv.at[peer], peer)

    def pass_on(peer):
        arrival(peer).wait_recv()
        for copy in relay(mine.at[peer], peer):
            copy.start()

    for_peers(pass_on)

    def take_coeffs(place, source):
        held = pl.ds(place * width, width)
        along[held] = source[0]
        across[held] = source[1]
        factors, inverse = factor_vertical(source[2])
        scale[held] = inverse
        for step, (alpha, gamma) in enumerate(factors):
            alphas[step, held] = alpha
            gammas[step, held] = gamma

    def take_observations(block, source):
        turned = source[...].reshape(slots, source.shape[2]).astype(jnp.float32).T
        weights[block] = turned[:depth].astype(jnp.bfloat16)
        column = turned[depth + 2 : depth + 3] * 16.0 + turned[depth + 3 : depth + 4]
        hits[block] = hit_matrix(column, width * nlat)
        if block == 1:
            precision[...] = turned[depth : depth + 1]
        return turned[depth : depth + 1] * turned[depth + 1 : depth + 2]

    take_coeffs(1, coeffs)
    start_mine = take_observations(1, mine)
    for copy in coeff_copies:
        copy.wait()
    take_coeffs(0, coeffs_low)
    take_coeffs(2, coeffs_high)
    for copy in relay(mine.at[me], me):
        copy.wait()

    def relayed(peer):
        for copy in relay(mine.at[peer], peer):
            copy.wait()

    for_peers(relayed)
    for_peers(lambda peer: arrival(peer).wait_send())
    start_low = take_observations(0, low)
    start_high = take_observations(2, high)
    spread_out((start_low, start_mine, start_high), weights, hits, field, width)
    norm[...] = jnp.zeros_like(norm)

    def first_stage(index, carry):
        part = pl.ds(pl.multiple_of(index * levels, levels), levels)
        solved = solve_vertical(alphas, gammas, scale, field[:, part, :], 0)
        own = smooth(along, across, solved, 0)
        rhs[:, part, :] = own
        inner = own[STEPS : STEPS + width]
        norm[...] += jnp.sum(inner * inner, axis=0)
        rhs_root[:, part, :] = solve_vertical(
            alphas, gammas, scale, smooth(along, across, own, STEPS), width
        )
        return carry

    lax.fori_loop(0, VARS, first_stage, 0)
    seen = forward(weights, hits, rhs_root)
    weighted = precision[...] * seen
    z_out[...] = weighted
    z_copies = to_sides(z_out, z_low, z_high, 2)
    for copy in z_copies:
        copy.start()
    sums_out[0:1, :] = total(norm[...], nlat)
    sums_out[1:2, :] = total(weighted * seen, nlat)
    sums_out[2:8, :] = jnp.zeros((6, nlat), jnp.float32)

    def sums_to(peer):
        return remote(sums_out, sums_in.at[me], sums_send.at[peer], sums_recv.at[me], peer)

    def sums_from(peer):
        return remote(sums_out, sums_in.at[peer], sums_send.at[peer], sums_recv.at[peer], peer)

    for_peers(lambda peer: sums_to(peer).start())
    sums_in[me] = sums_out[...]
    for row in range(rows):
        last_out[row : row + 1, :] = seen[:, row * nlat : (row + 1) * nlat]
    for copy in z_copies:
        copy.wait()
    spread_out((z_low[...], weighted, z_high[...]), weights, hits, field, width)
    for_peers(lambda peer: sums_from(peer).wait())
    sums = jnp.sum(sums_in[...], axis=0)
    first, fit = sums[0:1], sums[1:2]
    alpha = first / (first + fit)
    norm[...] = jnp.zeros_like(norm)
    cross[...] = jnp.zeros_like(cross)

    def second_stage(index, carry):
        part = pl.ds(pl.multiple_of(index * levels, levels), levels)
        solved = solve_vertical(alphas, gammas, scale, field[:, part, :], 0)
        start = rhs[:, part, :]
        image = start + smooth(along, across, solved, 0)
        left = start - alpha[None] * image
        inner = left[STEPS : STEPS + width]
        residual[:, part, :] = inner
        norm[...] += jnp.sum(inner * inner, axis=0)
        cross[...] += jnp.sum(inner * start[STEPS : STEPS + width], axis=0)
        residual_root[:, part, :] = solve_vertical(
            alphas, gammas, scale, smooth(along, across, left, STEPS), width
        )
        return carry

    lax.fori_loop(0, VARS, second_stage, 0)
    seen_rhs = seen
    seen = forward(weights, hits, residual_root)
    weighted = precision[...] * seen
    for row in range(rows):
        last_out[rows + row : rows + row + 1, :] = seen[:, row * nlat : (row + 1) * nlat]
    base = 2 * rows
    last_out[base : base + 1, :] = total(norm[...], nlat)
    last_out[base + 1 : base + 2, :] = total(cross[...], nlat)
    last_out[base + 2 : base + 3, :] = total(weighted * seen, nlat)
    last_out[base + 3 : base + 4, :] = total(weighted * seen_rhs, nlat)
    last_out[base + 4 : base + 8, :] = jnp.zeros((4, nlat), jnp.float32)

    def last_to(peer):
        return remote(last_out, last_in.at[me], last_send.at[peer], last_recv.at[me], peer)

    def last_from(peer):
        return remote(last_out, last_in.at[peer], last_send.at[peer], last_recv.at[peer], peer)

    for_peers(lambda peer: last_to(peer).start())
    last_in[me] = last_out[...]
    for_peers(lambda peer: last_from(peer).wait())
    sums = jnp.sum(last_in[:, base : base + 8, :], axis=0)
    fresh, mixed, fit_fresh, fit_mixed = sums[0:1], sums[1:2], sums[2:3], sums[3:4]
    beta = fresh / first
    curve = fresh + fit_fresh + 2.0 * beta * (mixed + fit_mixed) + beta * beta * (first + fit)
    on_residual = fresh / curve
    on_rhs = alpha + on_residual * beta

    def combine(index, carry):
        part = pl.ds(pl.multiple_of(index * levels, levels), levels)
        own = rhs[STEPS : STEPS + width, part, :]
        control[:, part, :] = on_rhs[None] * own + on_residual[None] * residual[:, part, :]
        increment[:, part, :] = (
            on_rhs[None] * rhs_root[:, part, :] + on_residual[None] * residual_root[:, part, :]
        )
        return carry

    lax.fori_loop(0, VARS, combine, 0)
    last_in[me, base + 4 : base + 5, :] = on_rhs
    last_in[me, base + 5 : base + 6, :] = on_residual


def on_device(
    obs_departure,
    obs_precision,
    obs_columns,
    obs_counts,
    obs_blocks,
    weight_table,
    lon_coeff,
    lat_coeff,
    vert_coeff,
):
    devices = lax.axis_size("lon")
    me = lax.axis_index("lon")
    levels, width, nlat = lon_coeff.shape
    percol = width * nlat
    depth = VARS * LEV
    per_dev = obs_columns.shape[0]
    capacity = max(per_dev // 64, 2 * ((per_dev + devices - 1) // devices), 16)
    slots_all = devices * capacity
    bf16, f32 = jnp.bfloat16, jnp.float32

    open_face = jnp.arange(nlat) < nlat - 1
    coeffs = jnp.stack([lon_coeff, jnp.where(open_face, lat_coeff, 0.0), vert_coeff])
    coeffs = coeffs.transpose(0, 2, 1, 3)

    slot = jnp.arange(per_dev, dtype=jnp.int32)
    live = slot < obs_counts[0]
    owner = obs_columns // percol
    local_col = obs_columns - owner * percol
    hits = (owner[:, None] == jnp.arange(devices, dtype=jnp.int32)) & live[:, None]
    before = jnp.dot(
        (slot[:, None] > slot).astype(bf16), hits.astype(bf16), preferred_element_type=f32
    )
    rank = jnp.sum(jnp.where(hits, before, 0.0), axis=1).astype(jnp.int32)
    target = jnp.where(live, owner * capacity + rank, slots_all)
    place = jnp.arange(slots_all, dtype=jnp.int32)[:, None] == target
    rows = weight_table.shape[0]
    pick = (obs_blocks[:, None] == jnp.arange(rows, dtype=jnp.int32)).astype(bf16)
    block_rows = jnp.dot(pick, weight_table, preferred_element_type=f32).astype(bf16)
    extra = jnp.stack(
        [
            obs_precision,
            obs_departure,
            (local_col // 16).astype(bf16),
            (local_col % 16).astype(bf16),
        ],
        axis=1,
    )
    lanes = -(-(depth + 4) // 128) * 128
    payload = jnp.concatenate([block_rows, extra], axis=1)
    payload = jnp.pad(payload, ((0, 0), (0, lanes - depth - 4)))
    payload = jnp.dot(place.astype(bf16), payload, preferred_element_type=f32).astype(bf16)
    payload = payload.reshape(devices, capacity, lanes)
    wide = 3 * width
    steps = (levels - 1).bit_length()
    rows = slots_all // nlat
    vmem = pl.BlockSpec(memory_space=pltpu.VMEM)
    own_shape = jax.ShapeDtypeStruct((width, depth, nlat), f32)
    last_shape = (2 * rows + 8, nlat)

    def held(*dims, dtype=f32):
        return pltpu.VMEM(dims, dtype)

    dma = pltpu.SemaphoreType.DMA
    control, increment, last = pl.pallas_call(
        whole_kernel,
        out_shape=[own_shape, own_shape, jax.ShapeDtypeStruct((devices,) + last_shape, f32)],
        in_specs=[vmem] * 2,
        out_specs=[vmem] * 3,
        scratch_shapes=[
            held(3, width, levels, nlat),
            held(3, width, levels, nlat),
            held(devices, capacity, lanes, dtype=bf16),
            held(devices, capacity, lanes, dtype=bf16),
            held(devices, capacity, lanes, dtype=bf16),
            held(3, depth, slots_all, dtype=bf16),
            held(3, percol, slots_all, dtype=bf16),
            held(wide, levels, nlat),
            held(wide, levels, nlat),
            held(steps, wide, levels, nlat),
            held(steps, wide, levels, nlat),
            held(wide, levels, nlat),
            held(1, slots_all),
            held(wide, depth, nlat),
            held(width + 2 * STEPS, depth, nlat),
            held(width, depth, nlat),
            held(width, depth, nlat),
            held(width, depth, nlat),
            held(levels, nlat),
            held(levels, nlat),
            held(1, slots_all),
            held(1, slots_all),
            held(1, slots_all),
            held(8, nlat),
            held(devices, 8, nlat),
            held(*last_shape),
            dma((devices,)),
            dma((devices,)),
            dma((2, devices)),
            dma((2, devices)),
            dma((4,)),
            dma((4,)),
            dma((devices,)),
            dma((devices,)),
            dma((devices,)),
            dma((devices,)),
        ],
        compiler_params=pltpu.CompilerParams(
            collective_id=0, has_side_effects=True, vmem_limit_bytes=48 * 2**20
        ),
    )(coeffs, payload)
    on_rhs, on_residual = lax.dynamic_index_in_dim(last, me, 0, False)[2 * rows + 4 : 2 * rows + 6, 0]
    fits = on_rhs * last[:, :rows] + on_residual * last[:, rows : 2 * rows]
    fits = fits.reshape(devices, slots_all)
    fit = lax.dynamic_slice_in_dim(fits, me * capacity, capacity, axis=1)
    fit = jnp.dot(fit.reshape(1, slots_all), place.astype(f32), precision=EXACT)[0]
    obs_fit = jnp.where(live, fit - obs_departure.astype(f32), 0.0)

    def placed(field):
        return field.reshape(width, VARS, levels, nlat).transpose(1, 2, 0, 3)

    return placed(control), placed(increment), obs_fit


def solution(mesh):
    in_specs = (
        P(("member", "lon")),
        P("lon"),
        P("lon"),
        P("lon"),
        P("lon"),
        P("lon", None),
        P(None, "lon", None),
        P(None, "lon", None),
        P(None, "lon", None),
    )
    out_specs = (
        P("member", None, "lon", None),
        P("member", None, "lon", None),
        P(("member", "lon")),
    )
    return jax.shard_map(
        on_device, mesh=mesh, in_specs=in_specs, out_specs=out_specs, check_vma=False
    )
```

time: 102 us -> 58.6 us (0.57)
  Pallas kernels: 14.2 us -> 46.3 us
  starting transfers between devices: 24.8 us -> 0 us
  waiting for transfers between devices: 22.1 us -> 0 us
  local copies, waits for them, and re-layouts: 23.9 us -> 6.9 us
  between operations: 7.84 us -> 1.45 us
  other arithmetic: 5.61 us -> 2.68 us
  matrix products: 2.34 us -> 0.89 us
    pallas_call x2 -> x1, Pallas kernels: 14.2 us -> 46.3 us  [on_device(): pl.pallas_call(whole_kernel, out_shape=[own_shape, own_shape, jax.ShapeDt...]
    all_to_all x3 -> x0, waiting for transfers between devices: 18.6 us -> none  [the longest x1 8.3 us: on_device(): lax.all_to_all(payload, 'lon', split_axis=0, concat_axis=0, tiled=True)]
    all_to_all x3 -> x0, starting transfers between devices: 15.9 us -> none  [the longest x1 7.38 us: on_device(): lax.all_to_all(payload, 'lon', split_axis=0, concat_axis=0, tiled=True)]
    unnamed x52 -> x18, local copies, waits for them, and re-layouts: 18.7 us -> 3.66 us
    ppermute x4 -> x0, starting transfers between devices: 8.93 us -> none  [neighbours(): return (lax.ppermute(block, axis, up), lax.ppermute(block, axis, down))]
    ppermute x4 -> x0, waiting for transfers between devices: 3.46 us -> none  [neighbours(): return (lax.ppermute(block, axis, up), lax.ppermute(block, axis, down))]
  transfers between devices with their start and end apart: 7 -> 0, of which waited for: 4 -> 0; matrix products, arithmetic and copies ran while one was open for 3% -> 0% of each run, Pallas kernels for 0% -> 0%
where the time goes in v2:
time: 58.6 us; the launch traced here: 58.2 us
  Pallas kernels  46.3 us (79%)
  local copies, waits for them, and re-layouts  6.9 us (12%)
  other arithmetic  2.68 us (5%)
  between operations  1.45 us (2%)
  matrix products  0.89 us (2%)
    pallas_call x1, Pallas kernels, on_device(): pl.pallas_call(whole_kernel, out_shape=[own_shape, own_shape, jax.ShapeDt...  46.3 us
    unnamed x18, local copies, waits for them, and re-layouts  3.66 us
    reshape x2, local copies, waits for them, and re-layouts, placed(): return field.reshape(width, VARS, levels, nlat).transpose(1, 2, 0, 3)  2 us
    add x1, other arithmetic, on_device(): fits = on_rhs * last[:, :rows] + on_residual * last[:, rows:2 * rows]  1.31 us

profile of v2, /device:TPU:0, one launch (start us, length us, event | category | flops | bytes accessed | tf_op | source)
XLA Modules:
  0.0 58.2 jit_solution(15724255005222245177)
XLA Ops:
  0.6 0.0 copy-start
  0.6 0.7 %fusion.11 = (bf16[256]{0:T(256)(128)(2,1)S(1)}, s32[256]{0:T(256)S(1)}) fusion(s32[256]{0:T(256)} %param.11), kind=kLoop, calls=%fused_computation.39 | loop fusion | flops 7424 | bytes 2560 | tf_op jit(solution)/shard_map/convert_element_type | solution.py:365
  2.0 0.2 fusion
  2.2 0.0 copy-start.4
  2.2 0.7 %copy-done.4 = s32[256]{0:T(256)S(1)} copy-done((s32[256]{0:T(256)S(1)}, s32[256]{0:T(256)}, u32[]{:S(2)}) %copy-start.4) | copy-done | bytes 1048
  2.9 0.1 stack.34
  3.0 0.0 copy-start.6
  3.0 0.1 stack.35
  3.1 0.0 copy-done
  3.1 0.6 copy-done.6
  3.7 0.0 copy-start.7
  3.7 0.2 convolution_convert_fusion.1
  3.9 0.4 copy-done.7
  4.4 0.1 stack.32
  4.5 0.6 copy-done.5
  5.0 0.1 stack.33
  5.1 0.2 concatenate.3
  5.3 0.0 copy-start.2
  5.3 0.0 copy-start.3
  5.3 0.2 convolution_convert_fusion
  5.6 0.6 copy-done.2
  6.1 0.0 copy-done.3
  6.2 0.8 %copy-done.1 = f32[32,4,128]{2,1,0:T(4,128)S(1)} copy-done((f32[32,4,128]{2,1,0:T(4,128)S(1)}, f32[32,4,128]{2,1,0:T(4,128)}, u32[]{:S(2)}) %copy-start.1) | copy-done | bytes 65560
  7.0 46.3 %shard_map.112 = (f32[4,192,128]{2,1,0:T(8,128)S(1)}, f32[4,192,128]{2,1,0:T(8,128)S(1)}, f32[16,16,128]{2,1,0:T(8,128)S(1)}) custom-call(f32[3,4,32,128]{3,2,1,0:T(8,128)S(1)} %maximum_bitcast_fusion.coeffs, bf16[16,32,256]{2,1,0:T(8,128)(2,1)S(1)} %bitcast.33), custom_call_target="tpu_custom_call" | custom-call | tf_op jit(solution)/shard_map/pallas_call | solution.py:385
  53.4 0.5 fusion.14
  53.9 1.3 %multiply_add_fusion = f32[16,4,128]{2,1,0:T(4,128)S(1)} fusion(f32[16,16,128]{2,1,0:T(8,128)S(1)} %get-tuple-element.8, f32[]{:T(128)} %bitcast.12, f32[]{:T(128)} %bitcast.11), kind=kLoop, calls=%fused_computation.20 | loop fusion | flops 24576 | bytes 98312 | tf_op jit(solution)/shard_map/add | solution.py:433
  55.2 0.1 constant_dynamic-slice_fusion
  55.3 0.1 reshape.41
  55.4 0.2 fusion.1
  55.6 0.6 %subtract_select_fusion = f32[256]{0:T(256)} fusion(f32[256]{0:T(256)S(1)} %bitcast.41, bf16[256]{0:T(256)(128)(2,1)S(1)} %copy-done.5, s32[]{:T(128)} %bitcast.31), kind=kLoop, calls=%fused_computation.35 | loop fusion | flops 1024 | bytes 2564 | tf_op jit(solution)/shard_map/jit(_where)/select_n | solution.py:437
  56.2 1.0 %copy.35 = f32[4,6,32,128]{3,0,2,1:T(4,128)} copy(f32[4,6,32,128]{3,2,1,0:T(8,128)S(1)} %bitcast.35) | data formatting | bytes 786432 | tf_op jit(solution)/shard_map/reshape | solution.py:440
  57.2 1.0 %copy.36 = f32[4,6,32,128]{3,0,2,1:T(4,128)} copy(f32[4,6,32,128]{3,2,1,0:T(8,128)S(1)} %bitcast.34) | data formatting | bytes 786432 | tf_op jit(solution)/shard_map/reshape | solution.py:440
  (10 shorter events, 0.1 us)
Async XLA Ops:
  0.6 2.5 %copy-start = (bf16[64,192]{1,0:T(8,128)(2,1)S(1)}, bf16[64,192]{1,0:T(8,128)(2,1)}, u32[]{:S(2)}) copy-start(bf16[64,192]{1,0:T(8,128)(2,1)} %param.14) | copy-start | bytes 73732
  2.2 0.7 %copy-start.4 = (s32[256]{0:T(256)S(1)}, s32[256]{0:T(256)}, u32[]{:S(2)}) copy-start(s32[256]{0:T(256)} %param.11) | copy-start | bytes 3076
  3.0 0.7 %copy-start.6 = (s32[256]{0:T(256)S(1)}, s32[256]{0:T(256)}, u32[]{:S(2)}) copy-start(s32[256]{0:T(256)} %param.13) | copy-start | bytes 3076
  3.7 0.7 %copy-start.7 = (bf16[256]{0:T(256)(128)(2,1)S(1)}, bf16[256]{0:T(256)(128)(2,1)}, u32[]{:S(2)}) copy-start(bf16[256]{0:T(256)(128)(2,1)} %param.10) | copy-start | bytes 1540
  4.4 0.7 %copy-start.5 = (bf16[256]{0:T(256)(128)(2,1)S(1)}, bf16[256]{0:T(256)(128)(2,1)}, u32[]{:S(2)}) copy-start(bf16[256]{0:T(256)(128)(2,1)} %param.9) | copy-start | bytes 1540
  5.3 0.8 %copy-start.2 = (f32[32,4,128]{2,1,0:T(4,128)S(1)}, f32[32,4,128]{2,1,0:T(4,128)}, u32[]{:S(2)}) copy-start(f32[32,4,128]{2,1,0:T(4,128)} %param.17) | copy-start | bytes 196612
  5.3 0.9 %copy-start.3 = (f32[32,4,128]{2,1,0:T(4,128)S(1)}, f32[32,4,128]{2,1,0:T(4,128)}, u32[]{:S(2)}) copy-start(f32[32,4,128]{2,1,0:T(4,128)} %param.16) | copy-start | bytes 196612
  6.2 0.8 %copy-start.1 = (f32[32,4,128]{2,1,0:T(4,128)S(1)}, f32[32,4,128]{2,1,0:T(4,128)}, u32[]{:S(2)}) copy-start(f32[32,4,128]{2,1,0:T(4,128)} %param.15) | copy-start | bytes 196612

commit v3 on v2

--- a/solution.py
+++ b/solution.py
@@ -8,7 +8,6 @@
 VARS = 6
 LEV = 32
 STEPS = 2
-EXACT = lax.Precision.HIGHEST
 
 
 def factor_vertical(vert):
@@ -103,15 +102,15 @@
 
 
 def whole_kernel(
-    coeffs, payload,
-    control, increment, last_in,
-    coeffs_low, coeffs_high, low, mine, high, weights, hits, along, across, alphas, gammas, scale,
+    departures, precisions, columns, counts, blocks, table, lon, lat, vert,
+    control, increment, obs_fit,
+    coeffs, payload, last_in, wide_table, extras, coeffs_low, coeffs_high, low, mine, high, weights, hits, along, across, alphas, gammas, scale,
     precision, field, rhs, rhs_root, residual, residual_root, norm, cross,
     z_out, z_low, z_high, sums_out, sums_in, last_out,
     pay_send, pay_recv, relay_send, relay_recv, side_send, side_recv, sums_send, sums_recv,
     last_send, last_recv,
 ):
-    devices = payload.shape[0]
+    devices, capacity, lanes = payload.shape
     me = lax.axis_index("lon")
     below, above = lax.rem(me + devices - 1, devices), lax.rem(me + 1, devices)
     width, levels, nlat = coeffs.shape[1:]
@@ -154,16 +153,57 @@
             barrier, inc=1, device_id={"lon": peer}, device_id_type=pl.DeviceIdType.MESH
         )
     )
+    for x in range(width):
+        coeffs[0, x] = lon[:, x, :]
+        across_own = lat[:, x, :]
+        face = lax.broadcasted_iota(jnp.int32, across_own.shape, 1)
+        coeffs[1, x] = jnp.where(face < nlat - 1, across_own, 0.0)
+        coeffs[2, x] = vert[:, x, :]
     pl.semaphore_wait(barrier, devices - 1)
+    coeff_copies = to_sides(coeffs, coeffs_low, coeffs_high, 0)
+    for copy in coeff_copies:
+        copy.start()
+
+    per_dev = columns.shape[1]
+    percol = float(width * nlat)
+    bf16, f32 = jnp.bfloat16, jnp.float32
+    live = lax.broadcasted_iota(jnp.int32, (1, per_dev), 1) < counts[0, 0]
+    column = columns[...].astype(f32)
+    owner = jnp.floor((column + 0.5) * (1.0 / percol))
+    local = column - owner * percol
+    local_high = jnp.floor((local + 0.5) * (1.0 / 16.0))
+    device_row = lax.broadcasted_iota(jnp.int32, (devices, per_dev), 0).astype(f32)
+    owned = jnp.where((device_row == owner) & live, 1.0, 0.0)
+    earlier = (
+        lax.broadcasted_iota(jnp.int32, (per_dev, per_dev), 0)
+        < lax.broadcasted_iota(jnp.int32, (per_dev, per_dev), 1)
+    )
+    earlier = jnp.where(earlier, 1.0, 0.0).astype(bf16)
+    before = matmul(owned.astype(bf16), earlier, ((1,), (0,)))
+    rank = jnp.sum(owned * before, axis=0, keepdims=True)
+    target = jnp.where(live, owner * float(capacity) + rank, float(slots))
+    slot_row = lax.broadcasted_iota(jnp.int32, (slots, per_dev), 0).astype(f32)
+    place = jnp.where(slot_row == target, 1.0, 0.0).astype(bf16)
+    table_row = lax.broadcasted_iota(jnp.int32, (table.shape[0], per_dev), 0)
+    pick = jnp.where(table_row == blocks[...], 1.0, 0.0).astype(bf16)
+    slot_pick = matmul(place, pick, ((1,), (1,))).astype(bf16)
+    wide_table[...] = jnp.zeros_like(wide_table)
+    wide_table[:, 0:depth] = table[...]
+    extras[...] = jnp.zeros_like(extras)
+    extras[depth : depth + 1, :] = precisions[...]
+    extras[depth + 1 : depth + 2, :] = departures[...]
+    extras[depth + 2 : depth + 3, :] = local_high
+    extras[depth + 3 : depth + 4, :] = local - local_high * 16.0
+    filled = matmul(slot_pick, wide_table[...], ((1,), (0,)))
+    filled += matmul(place, extras[...].astype(bf16), ((1,), (1,)))
+    payload[...] = filled.astype(bf16).reshape(devices, capacity, lanes)
+
 
     for_peers(
         lambda peer: remote(
             payload.at[peer], mine.at[me], pay_send.at[peer], pay_recv.at[me], peer
         ).start()
     )
-    coeff_copies = to_sides(coeffs, coeffs_low, coeffs_high, 0)
-    for copy in coeff_copies:
-        copy.start()
     mine[me] = payload[me]
     for copy in relay(mine.at[me], me):
         copy.start()
@@ -314,8 +354,15 @@
         return carry
 
     lax.fori_loop(0, VARS, combine, 0)
-    last_in[me, base + 4 : base + 5, :] = on_rhs
-    last_in[me, base + 5 : base + 6, :] = on_residual
+    begin = me * capacity
+    row = begin // nlat
+    lane = (begin - row * nlat).astype(f32) + rank
+    fits = on_rhs * last_in[:, row, :] + on_residual * last_in[:, rows + row, :]
+    lane_row = lax.broadcasted_iota(jnp.int32, (nlat, per_dev), 0).astype(f32)
+    at_lane = jnp.where(lane_row == lane, 1.0, 0.0).astype(bf16)
+    spread = sum(matmul(part, at_lane, ((1,), (0,))) for part in thirds(fits))
+    fit = jnp.sum(owned * spread, axis=0, keepdims=True)
+    obs_fit[...] = jnp.where(live, fit - departures[...], 0.0)
 
 
 def on_device(
@@ -330,7 +377,6 @@
     vert_coeff,
 ):
     devices = lax.axis_size("lon")
-    me = lax.axis_index("lon")
     levels, width, nlat = lon_coeff.shape
     percol = width * nlat
     depth = VARS * LEV
@@ -339,38 +385,7 @@
     slots_all = devices * capacity
     bf16, f32 = jnp.bfloat16, jnp.float32
 
-    open_face = jnp.arange(nlat) < nlat - 1
-    coeffs = jnp.stack([lon_coeff, jnp.where(open_face, lat_coeff, 0.0), vert_coeff])
-    coeffs = coeffs.transpose(0, 2, 1, 3)
-
-    slot = jnp.arange(per_dev, dtype=jnp.int32)
-    live = slot < obs_counts[0]
-    owner = obs_columns // percol
-    local_col = obs_columns - owner * percol
-    hits = (owner[:, None] == jnp.arange(devices, dtype=jnp.int32)) & live[:, None]
-    before = jnp.dot(
-        (slot[:, None] > slot).astype(bf16), hits.astype(bf16), preferred_element_type=f32
-    )
-    rank = jnp.sum(jnp.where(hits, before, 0.0), axis=1).astype(jnp.int32)
-    target = jnp.where(live, owner * capacity + rank, slots_all)
-    place = jnp.arange(slots_all, dtype=jnp.int32)[:, None] == target
-    rows = weight_table.shape[0]
-    pick = (obs_blocks[:, None] == jnp.arange(rows, dtype=jnp.int32)).astype(bf16)
-    block_rows = jnp.dot(pick, weight_table, preferred_element_type=f32).astype(bf16)
-    extra = jnp.stack(
-        [
-            obs_precision,
-            obs_departure,
-            (local_col // 16).astype(bf16),
-            (local_col % 16).astype(bf16),
-        ],
-        axis=1,
-    )
     lanes = -(-(depth + 4) // 128) * 128
-    payload = jnp.concatenate([block_rows, extra], axis=1)
-    payload = jnp.pad(payload, ((0, 0), (0, lanes - depth - 4)))
-    payload = jnp.dot(place.astype(bf16), payload, preferred_element_type=f32).astype(bf16)
-    payload = payload.reshape(devices, capacity, lanes)
     wide = 3 * width
     steps = (levels - 1).bit_length()
     rows = slots_all // nlat
@@ -382,12 +397,17 @@
         return pltpu.VMEM(dims, dtype)
 
     dma = pltpu.SemaphoreType.DMA
-    control, increment, last = pl.pallas_call(
+    control, increment, obs_fit = pl.pallas_call(
         whole_kernel,
-        out_shape=[own_shape, own_shape, jax.ShapeDtypeStruct((devices,) + last_shape, f32)],
-        in_specs=[vmem] * 2,
+        out_shape=[own_shape, own_shape, jax.ShapeDtypeStruct((1, per_dev), f32)],
+        in_specs=[vmem] * 3 + [pl.BlockSpec(memory_space=pltpu.SMEM)] + [vmem] * 5,
         out_specs=[vmem] * 3,
         scratch_shapes=[
+            held(3, width, levels, nlat),
+            held(devices, capacity, lanes, dtype=bf16),
+            held(devices, *last_shape),
+            held(weight_table.shape[0], lanes, dtype=bf16),
+            held(lanes, per_dev),
             held(3, width, levels, nlat),
             held(3, width, levels, nlat),
             held(devices, capacity, lanes, dtype=bf16),
@@ -428,18 +448,22 @@
         compiler_params=pltpu.CompilerParams(
             collective_id=0, has_side_effects=True, vmem_limit_bytes=48 * 2**20
         ),
-    )(coeffs, payload)
-    on_rhs, on_residual = lax.dynamic_index_in_dim(last, me, 0, False)[2 * rows + 4 : 2 * rows + 6, 0]
-    fits = on_rhs * last[:, :rows] + on_residual * last[:, rows : 2 * rows]
-    fits = fits.reshape(devices, slots_all)
-    fit = lax.dynamic_slice_in_dim(fits, me * capacity, capacity, axis=1)
-    fit = jnp.dot(fit.reshape(1, slots_all), place.astype(f32), precision=EXACT)[0]
-    obs_fit = jnp.where(live, fit - obs_departure.astype(f32), 0.0)
+    )(
+        obs_departure.astype(f32).reshape(1, per_dev),
+        obs_precision.astype(f32).reshape(1, per_dev),
+        obs_columns.reshape(1, per_dev),
+        obs_counts.reshape(1, 1),
+        obs_blocks.reshape(1, per_dev),
+        weight_table,
+        lon_coeff,
+        lat_coeff,
+        vert_coeff,
+    )
 
     def placed(field):
         return field.reshape(width, VARS, levels, nlat).transpose(1, 2, 0, 3)
 
-    return placed(control), placed(increment), obs_fit
+    return placed(control), placed(increment), obs_fit.reshape(per_dev)
 
 
 def solution(mesh):

time: 58.6 us -> 53.8 us (0.918)
  other arithmetic: 2.68 us -> 0.01 us
  Pallas kernels: 46.3 us -> 44.9 us
  matrix products: 0.89 us -> 0 us
    unnamed x18 -> x17, local copies, waits for them, and re-layouts: 3.66 us -> 5.83 us
    reshape x2 -> x0, local copies, waits for them, and re-layouts: 2 us -> none  [placed(): return field.reshape(width, VARS, levels, nlat).transpose(1, 2, 0, 3)]
    transpose x0 -> x1, local copies, waits for them, and re-layouts: none -> 1.39 us  [placed(): return field.reshape(width, VARS, levels, nlat).transpose(1, 2, 0, 3)]
    pallas_call x1, Pallas kernels: 46.3 us -> 44.9 us  [on_device(): pl.pallas_call(whole_kernel, out_shape=[own_shape, own_shape, jax.ShapeDt...]
    add x1 -> x0, other arithmetic: 1.31 us -> none  [on_device(): fits = on_rhs * last[:, :rows] + on_residual * last[:, rows:2 * rows]]
    another operation x6 -> x0, local copies, waits for them, and re-layouts: 0.98 us -> none  [the longest x1 0.52 us: on_device(): on_rhs, on_residual = lax.dynamic_index_in_dim(last, me, 0, False)[2 * ro...]
    dot_general x4 -> x0, matrix products: 0.89 us -> none  [the longest x1 0.24 us: on_device(): jnp.dot(place.astype(bf16), payload, preferred_element_type=f32)]
    convert_element_type x2 -> x0, other arithmetic: 0.72 us -> none  [the longest x1 0.7 us: on_device(): (local_col % 16).astype(bf16)]
where the time goes in v3:
time: 53.8 us; the launch traced here: 53.5 us
  Pallas kernels  44.9 us (83%)
  local copies, waits for them, and re-layouts  7.22 us (13%)
  between operations  1.3 us (2%)
    pallas_call x1, Pallas kernels, on_device(): pl.pallas_call(whole_kernel, out_shape=[own_shape, own_shape, jax.ShapeDt...  44.9 us
    unnamed x17, local copies, waits for them, and re-layouts  5.83 us
    transpose x1, local copies, waits for them, and re-layouts, placed(): return field.reshape(width, VARS, levels, nlat).transpose(1, 2, 0, 3)  1.39 us

profile of v3, /device:TPU:0, one launch (start us, length us, event | category | flops | bytes accessed | tf_op | source)
XLA Modules:
  0.0 53.5 jit_solution(422446011358823075)
XLA Ops:
  1.3 0.0 copy-start.6
  1.3 0.6 %copy-done.6 = bf16[256]{0:T(256)(128)(2,1)S(1)} copy-done((bf16[256]{0:T(256)(128)(2,1)S(1)}, bf16[256]{0:T(256)(128)(2,1)}, u32[]{:S(2)}) %copy-start.6) | copy-done | bytes 536
  1.9 0.0 copy-start.7
  1.9 0.7 %copy-done.7 = bf16[256]{0:T(256)(128)(2,1)S(1)} copy-done((bf16[256]{0:T(256)(128)(2,1)S(1)}, bf16[256]{0:T(256)(128)(2,1)}, u32[]{:S(2)}) %copy-start.7) | copy-done | bytes 536
  2.6 0.0 copy-start.5
  2.6 0.0 copy-start.4
  2.6 0.7 %copy-done.5 = s32[256]{0:T(256)S(1)} copy-done((s32[256]{0:T(256)S(1)}, s32[256]{0:T(256)}, u32[]{:S(2)}) %copy-start.5) | copy-done | bytes 1048
  3.3 0.0 copy-done.4
  3.3 0.0 copy-start
  3.3 0.8 %copy-done = f32[32,4,128]{2,1,0:T(4,128)S(1)} copy-done((f32[32,4,128]{2,1,0:T(4,128)S(1)}, f32[32,4,128]{2,1,0:T(4,128)}, u32[]{:S(2)}) %copy-start) | copy-done | bytes 65560
  4.1 0.0 copy-start.1
  4.1 0.8 %copy-done.1 = f32[32,4,128]{2,1,0:T(4,128)S(1)} copy-done((f32[32,4,128]{2,1,0:T(4,128)S(1)}, f32[32,4,128]{2,1,0:T(4,128)}, u32[]{:S(2)}) %copy-start.1) | copy-done | bytes 65560
  5.0 0.0 copy-start.2
  5.0 0.8 %copy-done.2 = f32[32,4,128]{2,1,0:T(4,128)S(1)} copy-done((f32[32,4,128]{2,1,0:T(4,128)S(1)}, f32[32,4,128]{2,1,0:T(4,128)}, u32[]{:S(2)}) %copy-start.2) | copy-done | bytes 65560
  5.8 0.0 copy-start.3
  5.8 0.8 %copy-done.3 = bf16[64,192]{1,0:T(8,128)(2,1)S(1)} copy-done((bf16[64,192]{1,0:T(8,128)(2,1)S(1)}, bf16[64,192]{1,0:T(8,128)(2,1)}, u32[]{:S(2)}) %copy-start.3) | copy-done | bytes 24600
  6.6 44.9 %shard_map.112 = (f32[4,192,128]{2,1,0:T(8,128)S(1)}, f32[4,192,128]{2,1,0:T(8,128)S(1)}, f32[1,256]{1,0:T(1,128)S(1)}) custom-call(f32[1,256]{1,0:T(1,128)S(1)} %bitcast.17, f32[1,256]{1,0:T(1,128)S(1)} %bitcast.18, s32[1,256]{1,0:T(1,128)S(1)} %bitcast.15, s32[1,1]{1,0:T(1,128)} %bitcast.12.counts, s32[1,256]{1,0:T(1,128)S(1)} %bitcast.16, ...), custom_call_target="tpu_custom_call" | custom-call | tf_op jit(solution)/shard_map/pallas_call | solution.py:400
  51.5 1.4 %copy_bitcast_fusion = (f32[6,32,4,128]{3,2,1,0:T(4,128)}, f32[6,32,4,128]{3,2,1,0:T(4,128)}) fusion(f32[4,6,32,128]{3,2,1,0:T(8,128)S(1)} %bitcast.14, f32[4,6,32,128]{3,2,1,0:T(8,128)S(1)} %bitcast.13), kind=kLoop, calls=%fused_computation | loop fusion | bytes 1572864 | tf_op jit(solution)/shard_map/transpose | solution.py:464
  52.9 0.6 %copy.18 = f32[256]{0:T(256)} copy(f32[256]{0:T(256)S(1)} %bitcast.19) | data formatting | bytes 2048
  (2 shorter events, 0.0 us)
Async XLA Ops:
  1.3 0.7 %copy-start.6 = (bf16[256]{0:T(256)(128)(2,1)S(1)}, bf16[256]{0:T(256)(128)(2,1)}, u32[]{:S(2)}) copy-start(bf16[256]{0:T(256)(128)(2,1)} %param.9) | copy-start | bytes 1540
  1.9 0.7 %copy-start.7 = (bf16[256]{0:T(256)(128)(2,1)S(1)}, bf16[256]{0:T(256)(128)(2,1)}, u32[]{:S(2)}) copy-start(bf16[256]{0:T(256)(128)(2,1)} %param.10) | copy-start | bytes 1540
  2.6 0.7 %copy-start.5 = (s32[256]{0:T(256)S(1)}, s32[256]{0:T(256)}, u32[]{:S(2)}) copy-start(s32[256]{0:T(256)} %param.13) | copy-start | bytes 3076
  2.6 0.7 %copy-start.4 = (s32[256]{0:T(256)S(1)}, s32[256]{0:T(256)}, u32[]{:S(2)}) copy-start(s32[256]{0:T(256)} %param.11) | copy-start | bytes 3076
  3.3 0.8 %copy-start = (f32[32,4,128]{2,1,0:T(4,128)S(1)}, f32[32,4,128]{2,1,0:T(4,128)}, u32[]{:S(2)}) copy-start(f32[32,4,128]{2,1,0:T(4,128)} %lon.1) | copy-start | bytes 196612
  4.1 0.8 %copy-start.1 = (f32[32,4,128]{2,1,0:T(4,128)S(1)}, f32[32,4,128]{2,1,0:T(4,128)}, u32[]{:S(2)}) copy-start(f32[32,4,128]{2,1,0:T(4,128)} %lat.1) | copy-start | bytes 196612
  5.0 0.8 %copy-start.2 = (f32[32,4,128]{2,1,0:T(4,128)S(1)}, f32[32,4,128]{2,1,0:T(4,128)}, u32[]{:S(2)}) copy-start(f32[32,4,128]{2,1,0:T(4,128)} %vert.1) | copy-start | bytes 196612
  5.8 0.8 %copy-start.3 = (bf16[64,192]{1,0:T(8,128)(2,1)S(1)}, bf16[64,192]{1,0:T(8,128)(2,1)}, u32[]{:S(2)}) copy-start(bf16[64,192]{1,0:T(8,128)(2,1)} %table.1) | copy-start | bytes 73732

commit v4 on v3

--- a/solution.py
+++ b/solution.py
@@ -102,6 +102,7 @@
 
 
 def whole_kernel(
+    loads,
     departures, precisions, columns, counts, blocks, table, lon, lat, vert,
     control, increment, obs_fit,
     coeffs, payload, last_in, wide_table, extras, coeffs_low, coeffs_high, low, mine, high, weights, hits, along, across, alphas, gammas, scale,
@@ -153,6 +154,8 @@
             barrier, inc=1, device_id={"lon": peer}, device_id_type=pl.DeviceIdType.MESH
         )
     )
+    for copy in loads:
+        copy.wait()
     for x in range(width):
         coeffs[0, x] = lon[:, x, :]
         across_own = lat[:, x, :]
@@ -365,6 +368,18 @@
     obs_fit[...] = jnp.where(live, fit - departures[...], 0.0)
 
 
+def loading_kernel(*refs):
+    sources, rest = refs[:9], refs[9:-9]
+    targets, sems = refs[-9:-1], refs[-1]
+    targets = targets[:3] + (sources[3],) + targets[3:]
+    loads = [
+        pltpu.make_async_copy(sources[i], targets[i], sems.at[i]) for i in range(9) if i != 3
+    ]
+    for copy in loads:
+        copy.start()
+    whole_kernel(loads, *targets, *rest)
+
+
 def on_device(
     obs_departure,
     obs_precision,
@@ -390,6 +405,7 @@
     steps = (levels - 1).bit_length()
     rows = slots_all // nlat
     vmem = pl.BlockSpec(memory_space=pltpu.VMEM)
+    far = pl.BlockSpec(memory_space=pltpu.HBM)
     own_shape = jax.ShapeDtypeStruct((width, depth, nlat), f32)
     last_shape = (2 * rows + 8, nlat)
 
@@ -398,9 +414,9 @@
 
     dma = pltpu.SemaphoreType.DMA
     control, increment, obs_fit = pl.pallas_call(
-        whole_kernel,
+        loading_kernel,
         out_shape=[own_shape, own_shape, jax.ShapeDtypeStruct((1, per_dev), f32)],
-        in_specs=[vmem] * 3 + [pl.BlockSpec(memory_space=pltpu.SMEM)] + [vmem] * 5,
+        in_specs=[far] * 3 + [pl.BlockSpec(memory_space=pltpu.SMEM)] + [far] * 5,
         out_specs=[vmem] * 3,
         scratch_shapes=[
             held(3, width, levels, nlat),
@@ -444,6 +460,15 @@
             dma((devices,)),
             dma((devices,)),
             dma((devices,)),
+            held(1, per_dev),
+            held(1, per_dev),
+            held(1, per_dev, dtype=jnp.int32),
+            held(1, per_dev, dtype=jnp.int32),
+            held(*weight_table.shape, dtype=bf16),
+            held(levels, width, nlat),
+            held(levels, width, nlat),
+            held(levels, width, nlat),
+            dma((9,)),
         ],
         compiler_params=pltpu.CompilerParams(
             collective_id=0, has_side_effects=True, vmem_limit_bytes=48 * 2**20

time: 53.8 us -> 54.3 us (level)
  no operation moved by 1% of the time
where the time goes in v4:
time: 54.3 us; the launch traced here: 53.9 us
  Pallas kernels  45.4 us (84%)
  local copies, waits for them, and re-layouts  7.22 us (13%)
  between operations  1.3 us (2%)
    pallas_call x1, Pallas kernels, on_device(): pl.pallas_call(loading_kernel, out_shape=[own_shape, own_shape, jax.Shape...  45.4 us
    unnamed x17, local copies, waits for them, and re-layouts  5.83 us
    transpose x1, local copies, waits for them, and re-layouts, placed(): return field.reshape(width, VARS, levels, nlat).transpose(1, 2, 0, 3)  1.39 us

profile of v4, /device:TPU:0, one launch (start us, length us, event | category | flops | bytes accessed | tf_op | source)
XLA Modules:
  0.0 53.9 jit_solution(3726744394212544672)
XLA Ops:
  1.3 0.0 copy-start.6
  1.3 0.6 %copy-done.6 = bf16[256]{0:T(256)(128)(2,1)S(1)} copy-done((bf16[256]{0:T(256)(128)(2,1)S(1)}, bf16[256]{0:T(256)(128)(2,1)}, u32[]{:S(2)}) %copy-start.6) | copy-done | bytes 536
  1.9 0.0 copy-start.7
  1.9 0.7 %copy-done.7 = bf16[256]{0:T(256)(128)(2,1)S(1)} copy-done((bf16[256]{0:T(256)(128)(2,1)S(1)}, bf16[256]{0:T(256)(128)(2,1)}, u32[]{:S(2)}) %copy-start.7) | copy-done | bytes 536
  2.6 0.0 copy-start.5
  2.6 0.0 copy-start.4
  2.6 0.7 %copy-done.5 = s32[256]{0:T(256)S(1)} copy-done((s32[256]{0:T(256)S(1)}, s32[256]{0:T(256)}, u32[]{:S(2)}) %copy-start.5) | copy-done | bytes 1048
  3.3 0.0 copy-done.4
  3.3 0.0 copy-start
  3.3 0.8 %copy-done = f32[32,4,128]{2,1,0:T(4,128)S(1)} copy-done((f32[32,4,128]{2,1,0:T(4,128)S(1)}, f32[32,4,128]{2,1,0:T(4,128)}, u32[]{:S(2)}) %copy-start) | copy-done | bytes 65560
  4.1 0.0 copy-start.1
  4.1 0.8 %copy-done.1 = f32[32,4,128]{2,1,0:T(4,128)S(1)} copy-done((f32[32,4,128]{2,1,0:T(4,128)S(1)}, f32[32,4,128]{2,1,0:T(4,128)}, u32[]{:S(2)}) %copy-start.1) | copy-done | bytes 65560
  5.0 0.0 copy-start.2
  5.0 0.8 %copy-done.2 = f32[32,4,128]{2,1,0:T(4,128)S(1)} copy-done((f32[32,4,128]{2,1,0:T(4,128)S(1)}, f32[32,4,128]{2,1,0:T(4,128)}, u32[]{:S(2)}) %copy-start.2) | copy-done | bytes 65560
  5.8 0.0 copy-start.3
  5.8 0.8 %copy-done.3 = bf16[64,192]{1,0:T(8,128)(2,1)S(1)} copy-done((bf16[64,192]{1,0:T(8,128)(2,1)S(1)}, bf16[64,192]{1,0:T(8,128)(2,1)}, u32[]{:S(2)}) %copy-start.3) | copy-done | bytes 24600
  6.6 45.4 %shard_map.112 = (f32[4,192,128]{2,1,0:T(8,128)S(1)}, f32[4,192,128]{2,1,0:T(8,128)S(1)}, f32[1,256]{1,0:T(1,128)S(1)}) custom-call(f32[1,256]{1,0:T(1,128)S(1)} %bitcast.17, f32[1,256]{1,0:T(1,128)S(1)} %bitcast.18, s32[1,256]{1,0:T(1,128)S(1)} %bitcast.15, s32[1,1]{1,0:T(1,128)} %bitcast.12.refs_3_, s32[1,256]{1,0:T(1,128)S(1)} %bitcast.16, ...), custom_call_target="tpu_custom_call" | custom-call | tf_op jit(solution)/shard_map/pallas_call | solution.py:416
  52.0 1.4 %copy_bitcast_fusion = (f32[6,32,4,128]{3,2,1,0:T(4,128)}, f32[6,32,4,128]{3,2,1,0:T(4,128)}) fusion(f32[4,6,32,128]{3,2,1,0:T(8,128)S(1)} %bitcast.14, f32[4,6,32,128]{3,2,1,0:T(8,128)S(1)} %bitcast.13), kind=kLoop, calls=%fused_computation | loop fusion | bytes 1572864 | tf_op jit(solution)/shard_map/transpose | solution.py:489
  53.4 0.6 %copy.18 = f32[256]{0:T(256)} copy(f32[256]{0:T(256)S(1)} %bitcast.19) | data formatting | bytes 2048
  (2 shorter events, 0.0 us)
Async XLA Ops:
  1.3 0.7 %copy-start.6 = (bf16[256]{0:T(256)(128)(2,1)S(1)}, bf16[256]{0:T(256)(128)(2,1)}, u32[]{:S(2)}) copy-start(bf16[256]{0:T(256)(128)(2,1)} %param.9) | copy-start | bytes 1540
  1.9 0.7 %copy-start.7 = (bf16[256]{0:T(256)(128)(2,1)S(1)}, bf16[256]{0:T(256)(128)(2,1)}, u32[]{:S(2)}) copy-start(bf16[256]{0:T(256)(128)(2,1)} %param.10) | copy-start | bytes 1540
  2.6 0.7 %copy-start.5 = (s32[256]{0:T(256)S(1)}, s32[256]{0:T(256)}, u32[]{:S(2)}) copy-start(s32[256]{0:T(256)} %param.13) | copy-start | bytes 3076
  2.6 0.7 %copy-start.4 = (s32[256]{0:T(256)S(1)}, s32[256]{0:T(256)}, u32[]{:S(2)}) copy-start(s32[256]{0:T(256)} %param.11) | copy-start | bytes 3076
  3.3 0.8 %copy-start = (f32[32,4,128]{2,1,0:T(4,128)S(1)}, f32[32,4,128]{2,1,0:T(4,128)}, u32[]{:S(2)}) copy-start(f32[32,4,128]{2,1,0:T(4,128)} %refs_6_.1) | copy-start | bytes 196612
  4.1 0.8 %copy-start.1 = (f32[32,4,128]{2,1,0:T(4,128)S(1)}, f32[32,4,128]{2,1,0:T(4,128)}, u32[]{:S(2)}) copy-start(f32[32,4,128]{2,1,0:T(4,128)} %refs_7_.1) | copy-start | bytes 196612
  5.0 0.8 %copy-start.2 = (f32[32,4,128]{2,1,0:T(4,128)S(1)}, f32[32,4,128]{2,1,0:T(4,128)}, u32[]{:S(2)}) copy-start(f32[32,4,128]{2,1,0:T(4,128)} %refs_8_.1) | copy-start | bytes 196612
  5.8 0.8 %copy-start.3 = (bf16[64,192]{1,0:T(8,128)(2,1)S(1)}, bf16[64,192]{1,0:T(8,128)(2,1)}, u32[]{:S(2)}) copy-start(bf16[64,192]{1,0:T(8,128)(2,1)} %refs_5_.1) | copy-start | bytes 73732
